TPU v7x, 32 devices: a whole 2x2x4 slice. The times are simulated.
32 devices in a mesh: replica: 8 (over z, x), group: 4 (over y, core).
Axes of the slice: x: 2, y: 2, z: 4, core: 2. Of those that a mesh axis runs over, the one named last changes fastest.
Arguments:
- images: bfloat16 [160, 197, 768], P(('replica', 'group')), may hold values from -6 to 6
- counts: int32 [32], P(('replica', 'group')), may hold values from 1 to 5, as said below
- ln1_gain: bfloat16 [768], P('group'), may hold values from 0.099609375 to 1.8984375
- ln1_shift: bfloat16 [768], P('group'), may hold values from -1.75 to 1.75
- w_qkv: bfloat16 [768, 2304], P('group'), may hold values from -0.21875 to 0.21875
- b_query: bfloat16 [768], P('group'), may hold values from -3 to 3
- b_value: bfloat16 [768], P('group'), may hold values from -3 to 3
- w_out: bfloat16 [768, 768], P('group'), may hold values from -1.75 to 1.75
- b_out: bfloat16 [768], P('group'), may hold values from -3 to 3
- ln2_gain: bfloat16 [768], P('group'), may hold values from 0.099609375 to 1.8984375
- ln2_shift: bfloat16 [768], P('group'), may hold values from -1.75 to 1.75
- w_up: bfloat16 [768, 3072], P('group'), may hold values from -0.21875 to 0.21875
- b_up: bfloat16 [3072], P('group'), may hold values from -3 to 3
- w_down: bfloat16 [3072, 768], P('group'), may hold values from -0.109375 to 0.109375
- b_down: bfloat16 [768], P('group'), may hold values from -3 to 3
- cotangent: bfloat16 [160, 197, 768], P(('replica', 'group')), may hold values from -6 to 6
Outputs:
- activations: bfloat16 [160, 197, 768], P(('replica', 'group'))
- input_grad: float32 [160, 197, 768], P(('replica', 'group'))
- grad_ln1_gain: float32 [768], P('group')
- grad_ln1_shift: float32 [768], P('group')
- grad_w_qkv: float32 [768, 2304], P('group')
- grad_b_query: float32 [768], P('group')
- grad_b_value: float32 [768], P('group')
- grad_w_out: float32 [768, 768], P('group')
- grad_b_out: float32 [768], P('group')
- grad_ln2_gain: float32 [768], P('group')
- grad_ln2_shift: float32 [768], P('group')
- grad_w_up: float32 [768, 3072], P('group')
- grad_b_up: float32 [3072], P('group')
- grad_w_down: float32 [3072, 768], P('group')
- grad_b_down: float32 [768], P('group')
Inputs may be any that keep to these rules, and one draw needn't show every extreme that they name: counts[d] is the number of live image slots of device d, slots 0 to counts[d] - 1; some device has all 5 live in every draw.
All inputs are finite; a program needn't handle non-finite values.
Results may differ from a plain program's by a relative error of at most 0.015.
Values may be sent and summed in bfloat16 or wider, within the bound.
No kernel may reach another device: no remote copies, remote signals or barrier semaphores. Data moves between devices by JAX's collectives and lax.ppermute only.
A program may use at most 192 MiB of HBM per device.

v0:
```python
import jax
import jax.numpy as jnp
from jax import lax
from jax.sharding import PartitionSpec as P

HEADS = 12


def layer_norm(field, gain, shift):
    centred = field - jnp.mean(field, -1, keepdims=True)
    spread = jnp.mean(centred * centred, -1, keepdims=True)
    return centred * lax.rsqrt(spread + 1e-06) * gain + shift


def smooth(field):
    return jax.nn.gelu(field, approximate=True)


def on_device(
    images,
    counts,
    ln1_gain,
    ln1_shift,
    w_qkv,
    b_query,
    b_value,
    w_out,
    b_out,
    ln2_gain,
    ln2_shift,
    w_up,
    b_up,
    w_down,
    b_down,
    cotangent,
):
    f32 = jnp.float32
    bf16 = jnp.bfloat16
    weights = (
        lax.all_gather(ln1_gain, "group", axis=0, tiled=True),
        lax.all_gather(ln1_shift, "group", axis=0, tiled=True),
        lax.all_gather(w_qkv, "group", axis=0, tiled=True),
        lax.all_gather(b_query, "group", axis=0, tiled=True),
        lax.all_gather(b_value, "group", axis=0, tiled=True),
        lax.all_gather(w_out, "group", axis=0, tiled=True),
        lax.all_gather(b_out, "group", axis=0, tiled=True),
        lax.all_gather(ln2_gain, "group", axis=0, tiled=True),
        lax.all_gather(ln2_shift, "group", axis=0, tiled=True),
        lax.all_gather(w_up, "group", axis=0, tiled=True),
        lax.all_gather(b_up, "group", axis=0, tiled=True),
        lax.all_gather(w_down, "group", axis=0, tiled=True),
        lax.all_gather(b_down, "group", axis=0, tiled=True),
    )
    slot_count, length, width = images.shape
    head_count = HEADS
    head_size = width // head_count
    factor = head_size ** (-0.5)
    live = (jnp.arange(slot_count, dtype=jnp.int32) < counts[0]).astype(f32)[:, None, None]
    inputs = images.astype(f32)
    gain_one = weights[0].astype(f32)
    shift_one = weights[1].astype(f32)
    gain_two = weights[7].astype(f32)
    shift_two = weights[8].astype(f32)
    normed_one, pull_one = jax.vjp(layer_norm, inputs, gain_one, shift_one)
    low_one = normed_one.astype(bf16)
    bias_cat = jnp.concatenate([weights[3], jnp.zeros_like(weights[3]), weights[4]]).astype(f32)
    packed = (
        jnp.einsum("bsd,de->bse", low_one, weights[2], preferred_element_type=f32) + bias_cat
    ).astype(bf16)
    query = packed[..., :width].reshape(slot_count, length, head_count, head_size)
    keys_low = packed[..., width : 2 * width].reshape(slot_count, length, head_count, head_size)
    values_low = packed[..., 2 * width :].reshape(slot_count, length, head_count, head_size)
    scores = jnp.einsum("bqhe,bkhe->bhqk", query, keys_low, preferred_element_type=f32) * factor
    top = jnp.max(scores, -1, keepdims=True)
    expo = jnp.exp(scores - top)
    total = jnp.sum(expo, -1, keepdims=True)
    log_total = top + jnp.log(total)
    probs_low = (expo / total).astype(bf16)
    attended = jnp.einsum("bhqk,bkhe->bqhe", probs_low, values_low, preferred_element_type=f32)
    attended = attended.reshape(slot_count, length, width).astype(bf16)
    middle = (
        inputs
        + jnp.einsum("bsd,de->bse", attended, weights[5], preferred_element_type=f32)
        + weights[6].astype(f32)
    )
    normed_two, pull_two = jax.vjp(layer_norm, middle, gain_two, shift_two)
    low_two = normed_two.astype(bf16)
    hidden_pre = jnp.einsum(
        "bsd,df->bsf", low_two, weights[9], preferred_element_type=f32
    ) + weights[10].astype(f32)
    hidden_act, pull_act = jax.vjp(smooth, hidden_pre)
    hidden_low = hidden_act.astype(bf16)
    branch_two = jnp.einsum(
        "bsf,fd->bsd", hidden_low, weights[11], preferred_element_type=f32
    ) + weights[12].astype(f32)
    outputs = ((middle + branch_two) * live).astype(bf16)
    again = (
        lax.all_gather(ln1_gain, "group", axis=0, tiled=True),
        lax.all_gather(ln1_shift, "group", axis=0, tiled=True),
        lax.all_gather(w_qkv, "group", axis=0, tiled=True),
        lax.all_gather(b_query, "group", axis=0, tiled=True),
        lax.all_gather(b_value, "group", axis=0, tiled=True),
        lax.all_gather(w_out, "group", axis=0, tiled=True),
        lax.all_gather(b_out, "group", axis=0, tiled=True),
        lax.all_gather(ln2_gain, "group", axis=0, tiled=True),
        lax.all_gather(ln2_shift, "group", axis=0, tiled=True),
        lax.all_gather(w_up, "group", axis=0, tiled=True),
        lax.all_gather(b_up, "group", axis=0, tiled=True),
        lax.all_gather(w_down, "group", axis=0, tiled=True),
        lax.all_gather(b_down, "group", axis=0, tiled=True),
    )
    proj_qkv, proj_out, proj_up, proj_down = (again[2], again[5], again[9], again[11])
    grad_out = cotangent.astype(f32) * live
    grad_low = grad_out.astype(bf16)
    grad_down = jnp.einsum("bsf,bsd->fd", hidden_low, grad_low, preferred_element_type=f32)
    grad_bdown = jnp.sum(grad_low.astype(f32), (0, 1))
    grad_hidden = jnp.einsum("bsd,fd->bsf", grad_low, proj_down, preferred_element_type=f32)
    grad_pre = pull_act(grad_hidden)[0].astype(bf16)
    grad_up = jnp.einsum("bsd,bsf->df", low_two, grad_pre, preferred_element_type=f32)
    grad_bup = jnp.sum(grad_pre.astype(f32), (0, 1))
    grad_normed = jnp.einsum("bsf,df->bsd", grad_pre, proj_up, preferred_element_type=f32)
    grad_mid_norm, grad_gain_two, grad_shift_two = pull_two(grad_normed)
    grad_middle = grad_out + grad_mid_norm
    grad_branch = grad_middle.astype(bf16)
    grad_proj_out = jnp.einsum("bsd,bse->de", attended, grad_branch, preferred_element_type=f32)
    grad_bout = jnp.sum(grad_branch.astype(f32), (0, 1))
    grad_att = jnp.einsum("bse,de->bsd", grad_branch, proj_out, preferred_element_type=f32).astype(
        bf16
    )
    grad_att = grad_att.reshape(slot_count, length, head_count, head_size)
    again_scores = (
        jnp.einsum("bqhe,bkhe->bhqk", query, keys_low, preferred_element_type=f32) * factor
    )
    again_probs = jnp.exp(again_scores - log_total)
    grad_value = jnp.einsum(
        "bhqk,bqhe->bkhe", again_probs.astype(bf16), grad_att, preferred_element_type=f32
    )
    grad_probs = jnp.einsum("bqhe,bkhe->bhqk", grad_att, values_low, preferred_element_type=f32)
    inner = jnp.sum(again_probs * grad_probs, -1, keepdims=True)
    grad_scores = (again_probs * (grad_probs - inner) * factor).astype(bf16)
    grad_query = jnp.einsum("bhqk,bkhe->bqhe", grad_scores, keys_low, preferred_element_type=f32)
    grad_key = jnp.einsum("bhqk,bqhe->bkhe", grad_scores, query, preferred_element_type=f32)
    grad_packed = jnp.concatenate(
        [
            grad_query.reshape(slot_count, length, width),
            grad_key.reshape(slot_count, length, width),
            grad_value.reshape(slot_count, length, width),
        ],
        -1,
    ).astype(bf16)
    grad_qkv = jnp.einsum("bsd,bse->de", low_one, grad_packed, preferred_element_type=f32)
    packed_sums = jnp.sum(grad_packed.astype(f32), (0, 1))
    grad_bquery = packed_sums[:width]
    grad_bvalue = packed_sums[2 * width :]
    grad_norm_one = jnp.einsum("bse,de->bsd", grad_packed, proj_qkv, preferred_element_type=f32)
    grad_in_norm, grad_gain_one, grad_shift_one = pull_one(grad_norm_one)
    input_grad = grad_middle + grad_in_norm
    shards = (
        lax.psum_scatter(
            grad_gain_one.astype(jnp.bfloat16), "group", scatter_dimension=0, tiled=True
        ).astype(jnp.float32),
        lax.psum_scatter(
            grad_shift_one.astype(jnp.bfloat16), "group", scatter_dimension=0, tiled=True
        ).astype(jnp.float32),
        lax.psum_scatter(
            grad_qkv.astype(jnp.bfloat16), "group", scatter_dimension=0, tiled=True
        ).astype(jnp.float32),
        lax.psum_scatter(
            grad_bquery.astype(jnp.bfloat16), "group", scatter_dimension=0, tiled=True
        ).astype(jnp.float32),
        lax.psum_scatter(
            grad_bvalue.astype(jnp.bfloat16), "group", scatter_dimension=0, tiled=True
        ).astype(jnp.float32),
        lax.psum_scatter(
            grad_proj_out.astype(jnp.bfloat16), "group", scatter_dimension=0, tiled=True
        ).astype(jnp.float32),
        lax.psum_scatter(
            grad_bout.astype(jnp.bfloat16), "group", scatter_dimension=0, tiled=True
        ).astype(jnp.float32),
        lax.psum_scatter(
            grad_gain_two.astype(jnp.bfloat16), "group", scatter_dimension=0, tiled=True
        ).astype(jnp.float32),
        lax.psum_scatter(
            grad_shift_two.astype(jnp.bfloat16), "group", scatter_dimension=0, tiled=True
        ).astype(jnp.float32),
        lax.psum_scatter(
            grad_up.astype(jnp.bfloat16), "group", scatter_dimension=0, tiled=True
        ).astype(jnp.float32),
        lax.psum_scatter(
            grad_bup.astype(jnp.bfloat16), "group", scatter_dimension=0, tiled=True
        ).astype(jnp.float32),
        lax.psum_scatter(
            grad_down.astype(jnp.bfloat16), "group", scatter_dimension=0, tiled=True
        ).astype(jnp.float32),
        lax.psum_scatter(
            grad_bdown.astype(jnp.bfloat16), "group", scatter_dimension=0, tiled=True
        ).astype(jnp.float32),
    )
    summed = lax.psum(
        (
            shards[0],
            shards[1],
            shards[2],
            shards[3],
            shards[4],
            shards[5],
            shards[6],
            shards[7],
            shards[8],
            shards[9],
            shards[10],
            shards[11],
            shards[12],
        ),
        "replica",
    )
    return (
        outputs,
        input_grad,
        summed[0],
        summed[1],
        summed[2],
        summed[3],
        summed[4],
        summed[5],
        summed[6],
        summed[7],
        summed[8],
        summed[9],
        summed[10],
        summed[11],
        summed[12],
    )


def solution(mesh):
    return jax.shard_map(
        on_device,
        mesh=mesh,
        in_specs=(
            P(("replica", "group"), None, None),
            P(("replica", "group")),
            P("group"),
            P("group"),
            P("group", None),
            P("group"),
            P("group"),
            P("group", None),
            P("group"),
            P("group"),
            P("group"),
            P("group", None),
            P("group"),
            P("group", None),
            P("group"),
            P(("replica", "group"), None, None),
        ),
        out_specs=(
            P(("replica", "group"), None, None),
            P(("replica", "group"), None, None),
            P("group"),
            P("group"),
            P("group", None),
            P("group"),
            P("group"),
            P("group", None),
            P("group"),
            P("group"),
            P("group"),
            P("group", None),
            P("group"),
            P("group", None),
            P("group"),
        ),
        check_vma=False,
    )
```

profile of v0, /device:TPU:0, one launch (start us, length us, event | category | flops | bytes accessed | tf_op | source)
XLA Modules:
  0.0 682.6 jit_solution(8180194309768224844)
XLA Ops:
  7.2 0.7 all-gather.6.cloned.1.call-update
  8.1 0.7 all-gather.8.cloned.1.call-update
  8.8 0.7 all-gather.10.cloned.1.call-update
  9.6 0.5 all-gather.12.cloned.1.call-update
  10.2 0.3 convert_reduce_fusion
  10.5 0.6 fusion.54
  11.8 0.6 fusion.96
  13.0 0.2 dynamic-update-slice
  13.3 0.2 dynamic-update-slice.1
  13.5 0.2 dynamic-update-slice.2
  13.7 0.2 dynamic-update-slice.3
  14.0 0.2 dynamic-update-slice.4
  14.2 0.2 dynamic-update-slice.5
  14.4 0.2 dynamic-update-slice.6
  14.7 13.2 %all-reduce.19 = (bf16[768]{0:T(1024)(128)(2,1)S(1)}, bf16[768]{0:T(1024)(128)(2,1)S(1)}, bf16[768]{0:T(1024)(128)(2,1)S(1)}, bf16[768]{0:T(1024)(128)(2,1)S(1)}...) all-reduce(bf16[768]{0:T(1024)(128)(2,1)S(1)} %dynamic-update-slice, ...), channel_id=1, replica_groups=mesh['replica'=8,'group'=4] {'group'}, use_global_device_ids=true, to_apply=%add.3 | all-reduce | flops 5376 | bytes 21504
  28.0 5.8 all-gather
  33.8 9.5 %all-gather.6.cloned.1.call-done = bf16[768,2304]{1,0:T(8,128)(2,1)} async-done(((bf16[192,2304]{1,0:T(8,128)(2,1)}), bf16[768,2304]{1,0:T(8,128)(2,1)}) %all-gather.6.cloned.1.call-update) | async-done | bytes 3538960 | tf_op jit(solution)/shard_map/all_gather | solution.py:42
  43.3 6.6 add_convert_fusion
  49.9 1.9 fusion.94
  51.8 3.9 copy.62
  55.8 2.2 copy.63
  58.0 2.6 copy.61
  60.6 4.7 multiply_reduce_fusion.1
  65.3 2.9 fusion.9
  68.3 1.4 copy-done
  69.7 0.3 copy-done.13
  70.0 4.1 fusion.58
  74.2 3.6 fusion.97
  77.8 1.6 copy-done.4
  79.4 0.5 multiply_reduce_fusion.4
  80.0 21.4 %all-gather.10.cloned.1.call-done = bf16[768,3072]{1,0:T(8,128)(2,1)} async-done(((bf16[192,3072]{1,0:T(8,128)(2,1)}), bf16[768,3072]{1,0:T(8,128)(2,1)}) %all-gather.10.cloned.1.call-update) | async-done | bytes 4718608 | tf_op jit(solution)/shard_map/all_gather | solution.py:49
  101.4 13.6 %fusion.38 = f32[5,197,3072]{2,1,0:T(8,128)} fusion(bf16[768,3072]{1,0:T(8,128)(2,1)} %all-gather.10.cloned.1.call-done, f32[5,197,768]{2,1,0:T(8,128)} %copy-done.4, f32[768]{0:T(1024)S(1)} %convert_element_type.173, f32[768]{0:T(1024)S(1)} %convert_element_type.172, f32[5,197]{1,0:T(8,128)S(1)} %fusion.77, f32[5,197]{1,0:T(8,128)S(1)} %broadcast_multiply_fusion), kind=kOutput, calls=%fused_computation.40 | convolution fusion | flops 4651595776 | bytes 19862216 | tf_op jit(solution)/shard_map/bsd,df->bsf/dot_general | solution.py:88
  115.0 25.4 %all-gather.12.cloned.1.call-done = bf16[3072,768]{1,0:T(8,128)(2,1)} async-done(((bf16[768,768]{1,0:T(8,128)(2,1)}), bf16[3072,768]{1,0:T(8,128)(2,1)}) %all-gather.12.cloned.1.call-update) | async-done | bytes 4718608 | tf_op jit(solution)/shard_map/all_gather | solution.py:51
  140.4 16.6 %fusion.98 = (bf16[3072]{0:T(1024)(128)(2,1)S(1)}, bf16[5,197,3072]{2,1,0:T(8,128)(2,1)S(1)}) fusion(f32[5,197,3072]{2,1,0:T(8,128)} %fusion.38, f32[3072]{0:T(1024)S(1)} %bitcast.86, bf16[3072,768]{1,0:T(8,128)(2,1)} %all-gather.12.cloned.1.call-done, bf16[5,197,768]{2,1,0:T(8,128)(2,1)S(1)} %copy-done.8, f32[5]{0:T(128)S(1)} %compare_convert_fusion), kind=kOutput, calls=%fused_computation.119 | convolution fusion | flops 4716649472 | bytes 24405524 | tf_op jit(solution)/shard_map/bsd,fd->bsf/dot_general | solution.py:117
  157.1 5.5 multiply_reduce_fusion.2
  162.6 1.1 fusion.93
  163.7 0.3 copy-done.9
  164.0 0.7 fusion.91
  164.7 1.1 copy-done.12
  165.8 2.6 bitcast_convert_fusion.3
  168.4 4.3 convolution_convert_fusion
  172.7 3.8 copy.66
  176.5 8.4 %fusion.99 = f32[5,12,197,197]{2,3,1,0:T(8,128)} fusion(bf16[5,197,12,64]{1,3,2,0:T(8,128)(2,1)} %bitcast.75, bf16[5,197,12,64]{1,3,2,0:T(8,128)(2,1)} %bitcast.78), kind=kOutput, calls=%fused_computation.120 | convolution fusion | flops 298053120 | bytes 12340080 | tf_op jit(solution)/shard_map/bqhe,bkhe->bhqk/dot_general | solution.py:138
  184.9 21.3 %fusion.62 = bf16[5,12,64,197]{3,2,1,0:T(8,128)(2,1)} fusion(bf16[5,197,12,64]{1,3,2,0:T(8,128)(2,1)} %bitcast.82, f32[5,12,197,197]{2,3,1,0:T(8,128)} %fusion.99, f32[5,12,197,197]{2,3,1,0:T(8,128)} %copy-done, f32[5,12,197]{2,1,0:T(8,128)S(1)} %log_add_fusion), kind=kOutput, calls=%fused_computation.75 | convolution fusion | flops 319778464 | bytes 21701520 | tf_op jit(solution)/shard_map/bhqk,bkhe->bqhe/dot_general | solution.py:141
  206.2 3.9 copy.70
  210.1 19.2 %fusion.65 = bf16[5,12,64,197]{3,2,1,0:T(8,128)(2,1)} fusion(bf16[5,197,12,64]{1,3,2,0:T(8,128)(2,1)} %bitcast.80, f32[5,12,197,197]{2,3,1,0:T(8,128)} %fusion.99, f32[5,12,197,197]{2,3,1,0:T(8,128)} %copy-done, f32[5,12,197]{2,1,0:T(8,128)S(1)} %log_add_fusion), kind=kOutput, calls=%fused_computation.76 | convolution fusion | flops 319778464 | bytes 21701520 | tf_op jit(solution)/shard_map/bhqk,bqhe->bkhe/dot_general | solution.py:142
  229.4 3.8 copy.71
  233.2 8.7 %fusion.59 = bf16[5,12,64,197]{3,2,1,0:T(8,128)(2,1)} fusion(bf16[5,197,12,64]{1,3,2,0:T(8,128)(2,1)} %bitcast.76, f32[5,12,197,197]{2,3,1,0:T(8,128)} %copy-done, f32[5,12,197]{2,1,0:T(8,128)S(1)} %log_add_fusion), kind=kOutput, calls=%fused_computation.74 | convolution fusion | flops 305795232 | bytes 12387360 | tf_op jit(solution)/shard_map/bhqk,bqhe->bkhe/dot_general | solution.py:135
  241.9 4.3 copy.72
  246.2 8.8 %bitcast_convert_fusion.2 = bf16[768,2304]{1,0:T(8,128)(2,1)} fusion(bf16[5,197,768]{2,1,0:T(8,128)(2,1)} %param.16, f32[768]{0:T(1024)S(1)} %convert_element_type.163, f32[768]{0:T(1024)S(1)} %convert_element_type.162, f32[5,197]{1,0:T(8,128)S(1)} %fusion.76, f32[5,197]{1,0:T(8,128)S(1)} %broadcast_multiply_fusion.1, bf16[5,197,768]{2,1,0:T(8,128)(2,1)} %copy.72, ...), kind=kOutput, calls=%fused_computation.25 | convolution fusion | flops 3505784832 | bytes 9604808 | tf_op jit(solution)/shard_map/bsd,bse->de/dot_general | solution.py:151
  255.0 10.3 %bitcast_convert_fusion.1 = bf16[768,3072]{1,0:T(8,128)(2,1)} fusion(bf16[5,197,3072]{2,1,0:T(8,128)(2,1)} %copy-done.31, f32[5,197,768]{2,1,0:T(8,128)} %copy-done.4, f32[768]{0:T(1024)S(1)} %convert_element_type.173, f32[768]{0:T(1024)S(1)} %convert_element_type.172, f32[5,197]{1,0:T(8,128)S(1)} %fusion.77, f32[5,197]{1,0:T(8,128)S(1)} %broadcast_multiply_fusion), kind=kOutput, calls=%fused_computation.20 | convolution fusion | flops 4653955072 | bytes 13810376 | tf_op jit(solution)/shard_map/bsd,bsf->df/dot_general | solution.py:119
  265.4 12.9 %bitcast_convert_fusion = bf16[3072,768]{1,0:T(8,128)(2,1)} fusion(bf16[5,197,768]{2,1,0:T(8,128)(2,1)} %param.31, f32[5]{0:T(128)S(1)} %compare_convert_fusion, f32[5,197,3072]{2,1,0:T(8,128)} %fusion.38, f32[3072]{0:T(1024)S(1)} %bitcast.87), kind=kOutput, calls=%fused_computation.19 | convolution fusion | flops 4682700800 | bytes 18347540 | tf_op jit(solution)/shard_map/bsf,bsd->fd/dot_general | solution.py:115
  279.6 0.2 dynamic-update-slice.7
  279.8 3.3 fusion.89
  283.1 0.5 copy-done.11
  283.6 6.5 fusion.90
  290.2 1.6 fusion.53
  291.8 10.8 %all-reduce.18 = (bf16[768]{0:T(1024)(128)(2,1)S(1)}, bf16[768]{0:T(1024)(128)(2,1)S(1)}, bf16[768]{0:T(1024)(128)(2,1)S(1)}, bf16[768]{0:T(1024)(128)(2,1)S(1)}...) all-reduce(bf16[768]{0:T(1024)(128)(2,1)S(1)} %dynamic-update-slice, ...), channel_id=1, replica_groups=mesh['replica'=8,'group'=4] {'group'}, use_global_device_ids=true, to_apply=%add.7 | all-reduce | flops 9984 | bytes 39936
  302.9 5.2 add_add_fusion.2
  308.1 0.7 copy-done.6
  308.8 13.5 %multiply_convert_fusion.2 = bf16[5,197,768]{2,1,0:T(8,128)(2,1)} fusion(f32[5,197,768]{2,1,0:T(8,128)S(1)} %copy-done.6, bf16[3072,768]{1,0:T(8,128)(2,1)} %all-gather.12.cloned.1.call-done, f32[5]{0:T(128)S(1)} %compare_convert_fusion, f32[768]{0:T(1024)S(1)} %convert_element_type.177, f32[5,197,3072]{2,1,0:T(8,128)} %fusion.38, f32[3072]{0:T(1024)S(1)} %bitcast.88), kind=kOutput, calls=%fused_computation.69 | convolution fusion | flops 4681099264 | bytes 21376532 | tf_op jit(solution)/shard_map/bsf,fd->bsd/dot_general | solution.py:93
  322.3 23.5 %reduce-scatter.9.cloned.1.call-done = bf16[192,3072]{1,0:T(8,128)(2,1)} async-done(((bf16[768,3072]{1,0:T(8,128)(2,1)}), bf16[192,3072]{1,0:T(8,128)(2,1)}) %reduce-scatter.9.cloned.1.call-update) | async-done | bytes 1179664 | tf_op jit(solution)/shard_map/reduce_scatter | solution.py:186
  345.9 50.6 %reduce-scatter.11.cloned.1.call-done = bf16[768,768]{1,0:T(8,128)(2,1)} async-done(((bf16[3072,768]{1,0:T(8,128)(2,1)}), bf16[768,768]{1,0:T(8,128)(2,1)}) %reduce-scatter.11.cloned.1.call-update) | async-done | bytes 1179664 | tf_op jit(solution)/shard_map/reduce_scatter | solution.py:192
  396.4 279.1 %all-reduce.21 = (f32[192]{0:T(256)}, f32[192]{0:T(256)}, f32[192,2304]{1,0:T(8,128)}, f32[192]{0:T(256)}, f32[192]{0:T(256)}, /*index=5*/f32[192,768]{1,0:T(8,1...) all-reduce(f32[192]{0:T(256)S(1)} %get-tuple-element.79, ...), channel_id=1, replica_groups=mesh['replica'=8,'group'=4] {'replica'}, use_global_device_ids=true, to_apply=%region_13.0 | all-reduce | flops 1771776 | bytes 10635264 | tf_op jit(solution)/shard_map/psum | solution.py:199
  (106 shorter events, 1.2 us)
Async XLA Ops:
  7.2 3.0 copy-start.1
  7.2 36.1 %all-gather.6.cloned.1.call-start = ((), (), s32[]{:S(2)}) async-start(), calls=%async_computation.4 | async-start | bytes 4423680 | tf_op jit(solution)/shard_map/all_gather | solution.py:42
  7.9 3.8 copy-start.19
  7.9 5.1 copy-start.22
  8.0 5.3 copy-start.23
  8.0 5.5 copy-start.24
  8.0 5.8 copy-start.25
  8.0 6.0 copy-start.26
  8.0 6.2 copy-start.27
  8.0 6.4 copy-start.28
  8.0 20.0 %copy-start.20 = (bf16[768]{0:T(1024)(128)(2,1)S(1)}, bf16[768]{0:T(1024)(128)(2,1)}, u32[]{:S(2)}) copy-start(bf16[768]{0:T(1024)(128)(2,1)} %param.28) | copy-start | bytes 4612
  8.0 66.2 %all-gather.8.cloned.1.call-start = ((), (), s32[]{:S(2)}) async-start(), calls=%async_computation.5 | async-start | bytes 1474560 | tf_op jit(solution)/shard_map/all_gather | solution.py:45
  8.8 92.7 %all-gather.10.cloned.1.call-start = ((), (), s32[]{:S(2)}) async-start(), calls=%async_computation.6 | async-start | bytes 5898240 | tf_op jit(solution)/shard_map/all_gather | solution.py:49
  9.5 130.9 %all-gather.12.cloned.1.call-start = ((), (), s32[]{:S(2)}) async-start(), calls=%async_computation.7 | async-start | bytes 5898240 | tf_op jit(solution)/shard_map/all_gather | solution.py:51
  10.1 312.3 %reduce-scatter.7.cloned.1.call-start = ((), (), s32[]{:S(2)}) async-start(), calls=%async_computation.9 | async-start | bytes 1474560 | tf_op jit(solution)/shard_map/reduce_scatter | solution.py:174
  11.1 32.3 %copy-start.17 = (f32[5,197]{1,0:T(8,128)}, f32[5,197]{1,0:T(8,128)S(1)}, u32[]{:S(2)}) copy-start(f32[5,197]{1,0:T(8,128)S(1)} %fusion.54) | copy-start | bytes 11824
  60.6 7.7 %copy-start.3 = (bf16[5,197,768]{1,2,0:T(8,128)(2,1)}, bf16[5,197,768]{1,2,0:T(8,128)(2,1)S(1)}, u32[]{:S(2)}) copy-start(bf16[5,197,768]{1,2,0:T(8,128)(2,1)S(1)} %copy.61) | copy-start | bytes 4538884
  65.3 4.4 copy-start
  65.3 4.7 copy-start.13
  68.3 1.8 copy-start.15
  77.8 1.7 copy-start.4
  77.8 2.2 copy-start.14
  77.8 2.2 copy-start.16
  80.0 60.4 %copy-start.8 = (bf16[5,197,768]{2,1,0:T(8,128)(2,1)S(1)}, bf16[5,197,768]{2,1,0:T(8,128)(2,1)}, u32[]{:S(2)}) copy-start(bf16[5,197,768]{2,1,0:T(8,128)(2,1)} %param.31) | copy-start | bytes 4538884
  140.4 16.6 %copy-start.5 = (f32[5,197,768]{2,1,0:T(8,128)S(1)}, f32[5,197,768]{2,1,0:T(8,128)}, u32[]{:S(2)}) copy-start(f32[5,197,768]{2,1,0:T(8,128)} %copy-done.4) | copy-start | bytes 9077764
  140.4 16.6 %copy-start.21 = (bf16[768,3072]{1,0:T(8,128)(2,1)S(1)}, bf16[768,3072]{1,0:T(8,128)(2,1)}, u32[]{:S(2)}) copy-start(bf16[768,3072]{1,0:T(8,128)(2,1)} %all-gather.10.cloned.1.call-done) | copy-start | bytes 14155780
  157.0 5.5 copy-start.31
  162.6 1.4 copy-start.9
  164.0 1.9 copy-start.30
  164.7 1.1 copy-start.12
  184.9 137.4 %reduce-scatter.5.cloned.1.call-start = ((), (), s32[]{:S(2)}) async-start(), calls=%async_computation.8 | async-start | bytes 4423680 | tf_op jit(solution)/shard_map/reduce_scatter | solution.py:165
  255.0 90.9 %reduce-scatter.9.cloned.1.call-start = ((), (), s32[]{:S(2)}) async-start(), calls=%async_computation.10 | async-start | bytes 5898240 | tf_op jit(solution)/shard_map/reduce_scatter | solution.py:186
  265.3 131.1 %reduce-scatter.11.cloned.1.call-start = ((), (), s32[]{:S(2)}) async-start(), calls=%async_computation.11 | async-start | bytes 5898240 | tf_op jit(solution)/shard_map/reduce_scatter | solution.py:192
  278.2 1.3 copy-start.29
  279.8 3.3 copy-start.2
  279.8 3.3 copy-start.10
  279.8 3.8 copy-start.11
  283.6 6.6 copy-start.18
  290.1 1.6 copy-start.7
  302.9 5.9 copy-start.6
Sparse Core Ops, SparseCore 0:
  9.6 33.6 all-gather.5
  44.9 17.4 all-gather.7
  64.0 37.4 all-gather.9
  102.9 37.5 all-gather.11
  185.0 25.7 reduce-scatter.6
  255.1 40.2 reduce-scatter.4
  298.0 47.8 reduce-scatter.8
  348.6 47.8 reduce-scatter.10
where the time goes:
time: 686 us; the launch traced here: 683 us
  blocking collectives  309 us (45%)
  matrix products  171 us (25%)
  waiting for transfers between devices  133 us (19%)
  local copies, waits for them, and re-layouts  35 us (5%)
  between operations  17.5 us (3%)
  other arithmetic  16.7 us (2%)
    psum x1, blocking collectives, on_device(): lax.psum((shards[0], shards[1], shards[2], shards[3], shards[4], shards[5...  279 us
    reduce_scatter x1, waiting for transfers between devices, on_device(): lax.psum_scatter(grad_down.astype(jnp.bfloat16), 'group', scatter_dimensi...  50.6 us
    all_gather x1, waiting for transfers between devices, on_device(): lax.all_gather(w_down, 'group', axis=0, tiled=True)  25.4 us
    unnamed x2, blocking collectives  24 us
    reduce_scatter x1, waiting for transfers between devices, on_device(): lax.psum_scatter(grad_up.astype(jnp.bfloat16), 'group', scatter_dimension...  23.5 us
    all_gather x1, waiting for transfers between devices, on_device(): lax.all_gather(w_up, 'group', axis=0, tiled=True)  21.4 us
    dot_general x1, matrix products, on_device(): jnp.einsum('bhqk,bkhe->bqhe', grad_scores, keys_low, preferred_element_ty...  21.3 us
    dot_general x1, matrix products, on_device(): jnp.einsum('bhqk,bqhe->bkhe', grad_scores, query, preferred_element_type=...  19.2 us
  transfers between devices with their start and end apart: 8, of which 5 were waited for; matrix products, arithmetic and copies ran while one was open for 25% of the time, Pallas kernels for 0%

commit v1 on v0

--- a/solution.py
+++ b/solution.py
@@ -1,3 +1,5 @@
+import functools
+
 import jax
 import jax.numpy as jnp
 from jax import lax
@@ -16,7 +18,88 @@
     return jax.nn.gelu(field, approximate=True)
 
 
+def swap(field, axis, size, bit):
+    return lax.ppermute(field, axis, [(at, at ^ bit) for at in range(size)])
+
+
+def is_power(size):
+    return size & (size - 1) == 0
+
+
+def pick(field, at, axis):
+    return lax.dynamic_index_in_dim(field, at, axis, keepdims=False)
+
+
+def gather_shards(shard, sizes):
+    groups, replicas = sizes
+    rows = shard.shape[0]
+    if groups != 4 or replicas % 2 or rows % 32:
+        return lax.all_gather(shard, "group", axis=0, tiled=True)
+    me = lax.axis_index("group")
+    half = lax.axis_index("replica") & 1
+    near = swap(shard, "group", 4, 1)
+    first = swap(pick(shard.reshape(2, rows // 2, -1), half, 0), "group", 4, 2)
+    second = swap(first, "replica", replicas, 1)
+    far_first = swap(first, "group", 4, 1)
+    far_second = swap(second, "group", 4, 1)
+    whole = jnp.zeros((4 * rows, shard.shape[1]), shard.dtype)
+
+    def put(whole, part, owner, at):
+        return lax.dynamic_update_slice(whole, part, (owner * rows + at * (rows // 2), 0))
+
+    whole = put(whole, shard, me, 0)
+    whole = put(whole, near, me ^ 1, 0)
+    whole = put(whole, first, me ^ 2, half)
+    whole = put(whole, second, me ^ 2, 1 - half)
+    whole = put(whole, far_first, me ^ 3, half)
+    return put(whole, far_second, me ^ 3, 1 - half)
+
+
+def add_low(left, right, kind):
+    return (left.astype(jnp.float32) + right.astype(jnp.float32)).astype(kind)
+
+
+def reduce_shards(grad, sizes, halvings):
+    groups, replicas = sizes
+    rows = grad.shape[0] // groups
+    kind = grad.dtype
+    if not (is_power(groups) and is_power(replicas)):
+        shard = lax.psum_scatter(grad, "group", scatter_dimension=0, tiled=True)
+        return lax.psum(shard.astype(jnp.float32), "replica")
+    me = lax.axis_index("group")
+    other = lax.axis_index("replica")
+    tail = grad.shape[1:]
+    field = grad.reshape((groups, rows) + tail)
+    bit = 1
+    while bit < groups:
+        side = (me // bit) & 1
+        pairs = field.reshape((field.shape[0] // 2, 2, rows) + tail)
+        came = swap(pick(pairs, 1 - side, 1), "group", groups, bit)
+        field = add_low(pick(pairs, side, 1), came, kind)
+        bit *= 2
+    field = field[0]
+    done = []
+    bit = 1
+    while bit < replicas:
+        side = (other // bit) & 1
+        if len(done) < halvings:
+            pairs = field.reshape((2, field.shape[0] // 2) + tail)
+            came = swap(pick(pairs, 1 - side, 0), "replica", replicas, bit)
+            field = add_low(pick(pairs, side, 0), came, kind)
+            done.append((bit, side))
+        else:
+            field = add_low(field, swap(field, "replica", replicas, bit), kind)
+        bit *= 2
+    for bit, side in reversed(done):
+        came = swap(field, "replica", replicas, bit)
+        field = jnp.where(
+            side == 0, jnp.concatenate([field, came]), jnp.concatenate([came, field])
+        )
+    return field.astype(jnp.float32)
+
+
 def on_device(
+    sizes,
     images,
     counts,
     ln1_gain,
@@ -36,20 +119,31 @@
 ):
     f32 = jnp.float32
     bf16 = jnp.bfloat16
+    vectors = (ln1_gain, ln1_shift, b_query, b_value, b_out, ln2_gain, ln2_shift, b_down, b_up)
+    row = jnp.concatenate(vectors)
+    rows = lax.all_gather(row, "group", axis=0, tiled=False)
+    ends = [0]
+    for vector in vectors:
+        ends.append(ends[-1] + vector.shape[0])
+    small = [rows[:, at:end].reshape(-1) for at, end in zip(ends, ends[1:])]
+    w_qkv = gather_shards(w_qkv, sizes)
+    w_out = gather_shards(w_out, sizes)
+    w_up = gather_shards(w_up, sizes)
+    w_down = gather_shards(w_down, sizes)
     weights = (
-        lax.all_gather(ln1_gain, "group", axis=0, tiled=True),
-        lax.all_gather(ln1_shift, "group", axis=0, tiled=True),
-        lax.all_gather(w_qkv, "group", axis=0, tiled=True),
-        lax.all_gather(b_query, "group", axis=0, tiled=True),
-        lax.all_gather(b_value, "group", axis=0, tiled=True),
-        lax.all_gather(w_out, "group", axis=0, tiled=True),
-        lax.all_gather(b_out, "group", axis=0, tiled=True),
-        lax.all_gather(ln2_gain, "group", axis=0, tiled=True),
-        lax.all_gather(ln2_shift, "group", axis=0, tiled=True),
-        lax.all_gather(w_up, "group", axis=0, tiled=True),
-        lax.all_gather(b_up, "group", axis=0, tiled=True),
-        lax.all_gather(w_down, "group", axis=0, tiled=True),
-        lax.all_gather(b_down, "group", axis=0, tiled=True),
+        small[0],
+        small[1],
+        w_qkv,
+        small[2],
+        small[3],
+        w_out,
+        small[4],
+        small[5],
+        small[6],
+        w_up,
+        small[8],
+        w_down,
+        small[7],
     )
     slot_count, length, width = images.shape
     head_count = HEADS
@@ -94,22 +188,7 @@
         "bsf,fd->bsd", hidden_low, weights[11], preferred_element_type=f32
     ) + weights[12].astype(f32)
     outputs = ((middle + branch_two) * live).astype(bf16)
-    again = (
-        lax.all_gather(ln1_gain, "group", axis=0, tiled=True),
-        lax.all_gather(ln1_shift, "group", axis=0, tiled=True),
-        lax.all_gather(w_qkv, "group", axis=0, tiled=True),
-        lax.all_gather(b_query, "group", axis=0, tiled=True),
-        lax.all_gather(b_value, "group", axis=0, tiled=True),
-        lax.all_gather(w_out, "group", axis=0, tiled=True),
-        lax.all_gather(b_out, "group", axis=0, tiled=True),
-        lax.all_gather(ln2_gain, "group", axis=0, tiled=True),
-        lax.all_gather(ln2_shift, "group", axis=0, tiled=True),
-        lax.all_gather(w_up, "group", axis=0, tiled=True),
-        lax.all_gather(b_up, "group", axis=0, tiled=True),
-        lax.all_gather(w_down, "group", axis=0, tiled=True),
-        lax.all_gather(b_down, "group", axis=0, tiled=True),
-    )
-    proj_qkv, proj_out, proj_up, proj_down = (again[2], again[5], again[9], again[11])
+    proj_qkv, proj_out, proj_up, proj_down = (w_qkv, w_out, w_up, w_down)
     grad_out = cotangent.astype(f32) * live
     grad_low = grad_out.astype(bf16)
     grad_down = jnp.einsum("bsf,bsd->fd", hidden_low, grad_low, preferred_element_type=f32)
@@ -155,64 +234,38 @@
     grad_norm_one = jnp.einsum("bse,de->bsd", grad_packed, proj_qkv, preferred_element_type=f32)
     grad_in_norm, grad_gain_one, grad_shift_one = pull_one(grad_norm_one)
     input_grad = grad_middle + grad_in_norm
-    shards = (
-        lax.psum_scatter(
-            grad_gain_one.astype(jnp.bfloat16), "group", scatter_dimension=0, tiled=True
-        ).astype(jnp.float32),
-        lax.psum_scatter(
-            grad_shift_one.astype(jnp.bfloat16), "group", scatter_dimension=0, tiled=True
-        ).astype(jnp.float32),
-        lax.psum_scatter(
-            grad_qkv.astype(jnp.bfloat16), "group", scatter_dimension=0, tiled=True
-        ).astype(jnp.float32),
-        lax.psum_scatter(
-            grad_bquery.astype(jnp.bfloat16), "group", scatter_dimension=0, tiled=True
-        ).astype(jnp.float32),
-        lax.psum_scatter(
-            grad_bvalue.astype(jnp.bfloat16), "group", scatter_dimension=0, tiled=True
-        ).astype(jnp.float32),
-        lax.psum_scatter(
-            grad_proj_out.astype(jnp.bfloat16), "group", scatter_dimension=0, tiled=True
-        ).astype(jnp.float32),
-        lax.psum_scatter(
-            grad_bout.astype(jnp.bfloat16), "group", scatter_dimension=0, tiled=True
-        ).astype(jnp.float32),
-        lax.psum_scatter(
-            grad_gain_two.astype(jnp.bfloat16), "group", scatter_dimension=0, tiled=True
-        ).astype(jnp.float32),
-        lax.psum_scatter(
-            grad_shift_two.astype(jnp.bfloat16), "group", scatter_dimension=0, tiled=True
-        ).astype(jnp.float32),
-        lax.psum_scatter(
-            grad_up.astype(jnp.bfloat16), "group", scatter_dimension=0, tiled=True
-        ).astype(jnp.float32),
-        lax.psum_scatter(
-            grad_bup.astype(jnp.bfloat16), "group", scatter_dimension=0, tiled=True
-        ).astype(jnp.float32),
-        lax.psum_scatter(
-            grad_down.astype(jnp.bfloat16), "group", scatter_dimension=0, tiled=True
-        ).astype(jnp.float32),
-        lax.psum_scatter(
-            grad_bdown.astype(jnp.bfloat16), "group", scatter_dimension=0, tiled=True
-        ).astype(jnp.float32),
-    )
-    summed = lax.psum(
-        (
-            shards[0],
-            shards[1],
-            shards[2],
-            shards[3],
-            shards[4],
-            shards[5],
-            shards[6],
-            shards[7],
-            shards[8],
-            shards[9],
-            shards[10],
-            shards[11],
-            shards[12],
-        ),
-        "replica",
+    big = [
+        reduce_shards(grad.astype(bf16), sizes, 2)
+        for grad in (grad_down, grad_up, grad_proj_out, grad_qkv)
+    ]
+    parts = (
+        grad_gain_one,
+        grad_shift_one,
+        grad_bquery,
+        grad_bvalue,
+        grad_bout,
+        grad_gain_two,
+        grad_shift_two,
+        grad_bdown,
+        grad_bup,
+    )
+    joined = jnp.concatenate([part.reshape(sizes[0], -1) for part in parts], 1)
+    little = reduce_shards(joined.reshape(sizes[0], -1, 128), sizes, 0).reshape(-1)
+    sums = [little[at:end] for at, end in zip(ends, ends[1:])]
+    summed = (
+        sums[0],
+        sums[1],
+        big[3],
+        sums[2],
+        sums[3],
+        big[2],
+        sums[4],
+        sums[5],
+        sums[6],
+        big[1],
+        sums[8],
+        big[0],
+        sums[7],
     )
     return (
         outputs,
@@ -234,8 +287,9 @@
 
 
 def solution(mesh):
+    sizes = (mesh.shape["group"], mesh.shape["replica"])
     return jax.shard_map(
-        on_device,
+        functools.partial(on_device, sizes),
         mesh=mesh,
         in_specs=(
             P(("replica", "group"), None, None),

time: 686 us -> 510 us (0.74)
  blocking collectives: 309 us -> 7.25 us
  local copies, waits for them, and re-layouts: 35 us -> 87.7 us
  starting transfers between devices: 0.32 us -> 51 us
  waiting for transfers between devices: 133 us -> 165 us
  between operations: 17.5 us -> 2.36 us
  other arithmetic: 16.7 us -> 28.4 us
  matrix products: 171 us -> 162 us
    psum x1 -> x0, blocking collectives: 279 us -> none  [on_device(): lax.psum((shards[0], shards[1], shards[2], shards[3], shards[4], shards[5...]
    ppermute x0 -> x53, waiting for transfers between devices: none -> 165 us  [swap(): return lax.ppermute(field, axis, [(at, at ^ bit) for at in range(size)])]
    reduce_scatter x4 -> x0, waiting for transfers between devices: 74.1 us -> none  [the longest x1 50.6 us: on_device(): lax.psum_scatter(grad_down.astype(jnp.bfloat16), 'group', scatter_dimensi...]
    all_gather x4 -> x0, waiting for transfers between devices: 56.4 us -> none  [the longest x1 25.4 us: on_device(): lax.all_gather(w_down, 'group', axis=0, tiled=True)]
    ppermute x0 -> x53, starting transfers between devices: none -> 51 us  [swap(): return lax.ppermute(field, axis, [(at, at ^ bit) for at in range(size)])]
    dynamic_update_slice x0 -> x24, local copies, waits for them, and re-layouts: none -> 30.7 us  [put(): lax.dynamic_update_slice(whole, part, (owner * rows + at * (rows // 2), 0))]
    unnamed x2 -> x0, blocking collectives: 24 us -> none
    squeeze x0 -> x22, local copies, waits for them, and re-layouts: none -> 11.9 us  [pick(): return lax.dynamic_index_in_dim(field, at, axis, keepdims=False)]
  transfers between devices with their start and end apart: 8 -> 53, of which waited for: 5 -> 24; matrix products, arithmetic and copies ran while one was open for 25% -> 26% of each run, Pallas kernels for 0% -> 0%
where the time goes in v1:
time: 510 us; the launch traced here: 504 us
  waiting for transfers between devices  165 us (32%)
  matrix products  162 us (32%)
  local copies, waits for them, and re-layouts  87.7 us (17%)
  starting transfers between devices  51 us (10%)
  other arithmetic  28.4 us (6%)
  blocking collectives  7.25 us (1%)
    ppermute x53, waiting for transfers between devices, swap(): return lax.ppermute(field, axis, [(at, at ^ bit) for at in range(size)])  165 us
    ppermute x53, starting transfers between devices, swap(): return lax.ppermute(field, axis, [(at, at ^ bit) for at in range(size)])  51 us
    dynamic_update_slice x24, local copies, waits for them, and re-layouts, put(): lax.dynamic_update_slice(whole, part, (owner * rows + at * (rows // 2), 0))  30.7 us
    dot_general x1, matrix products, on_device(): jnp.einsum('bhqk,bkhe->bqhe', grad_scores, keys_low, preferred_element_ty...  20.3 us
    dot_general x1, matrix products, on_device(): jnp.einsum('bhqk,bqhe->bkhe', grad_scores, query, preferred_element_type=...  19.2 us
    dot_general x1, matrix products, on_device(): jnp.einsum('bsd,fd->bsf', grad_low, proj_down, preferred_element_type=f32)  16.6 us
    dot_general x1, matrix products, on_device(): jnp.einsum('bsf,bsd->fd', hidden_low, grad_low, preferred_element_type=f32)  12.3 us
    squeeze x22, local copies, waits for them, and re-layouts, pick(): return lax.dynamic_index_in_dim(field, at, axis, keepdims=False)  11.9 us
  transfers between devices with their start and end apart: 53, of which 24 were waited for; matrix products, arithmetic and copies ran while one was open for 26% of the time, Pallas kernels for 0%

profile of v1, /device:TPU:0, one launch (start us, length us, event | category | flops | bytes accessed | tf_op | source)
XLA Modules:
  0.0 504.1 jit_solution(1141995645308172950)
XLA Ops:
  2.8 2.6 collective-permute-start.6
  7.8 6.1 %concatenate.69 = bf16[2304]{0:T(1024)(128)(2,1)S(1)} concatenate(bf16[192]{0:T(256)(128)(2,1)} %param.18, bf16[192]{0:T(256)(128)(2,1)} %param.19, bf16[192]{0:T(256)(128)(2,1)} %param.21, bf16[192]{0:T(256)(128)(2,1)} %param.22, bf16[192]{0:T(256)(128)(2,1)} %param.24, bf16[192]{0:T(256)(128)(2,1)} %param.25, bf16[192]{0:T(256)(128)(2,1)} %param.26, bf16[192]{0:T(256)(128)(2,1)} %param.30, ...), dimensions={0} | concatenate | bytes 9216 | tf_op jit(solution)/shard_map/concatenate | solution.py:123
  13.9 7.3 %all-gather.1 = bf16[4,1,2304]{2,1,0:T(2,128)(2,1)S(1)} all-gather(bf16[1,1,2304]{2,1,0:T(2,128)(2,1)S(1)} %reshape.388), channel_id=2, replica_groups=mesh['replica'=8,'group'=4] {'group'}, dimensions={0}, use_global_device_ids=true | all-gather | bytes 23040 | tf_op jit(solution)/shard_map/all_gather | solution.py:124
  27.1 2.1 broadcast_in_dim.18
  30.1 2.8 broadcast_in_dim.21
  37.9 2.4 broadcast_in_dim.22
  50.8 2.1 constant_dynamic-update-slice_fusion.22
  54.8 7.4 %collective-permute-done.11 = bf16[96,3072]{1,0:T(8,128)(2,1)S(1)} collective-permute-done((bf16[96,3072]{1,0:T(8,128)(2,1)S(1)}, bf16[96,3072]{1,0:T(8,128)(2,1)S(1)}, u32[]{:S(2)}, u32[]{:S(2)}) %collective-permute-start.11) | collective-permute-done | bytes 589856 | tf_op jit(solution)/shard_map/ppermute | solution.py:22
  63.5 10.4 %collective-permute-done.16 = bf16[384,768]{1,0:T(8,128)(2,1)S(1)} collective-permute-done((bf16[384,768]{1,0:T(8,128)(2,1)S(1)}, bf16[384,768]{1,0:T(8,128)(2,1)S(1)}, u32[]{:S(2)}, u32[]{:S(2)}) %collective-permute-start.16) | collective-permute-done | bytes 589856 | tf_op jit(solution)/shard_map/ppermute | solution.py:22
  76.7 2.4 constant_dynamic-update-slice_fusion.10
  79.9 10.3 %collective-permute-done.12 = bf16[96,3072]{1,0:T(8,128)(2,1)} collective-permute-done((bf16[96,3072]{1,0:T(8,128)(2,1)S(1)}, bf16[96,3072]{1,0:T(8,128)(2,1)}, u32[]{:S(2)}, u32[]{:S(2)}) %collective-permute-start.12) | collective-permute-done | bytes 589856 | tf_op jit(solution)/shard_map/ppermute | solution.py:22
  90.2 10.8 %collective-permute-done.17 = bf16[384,768]{1,0:T(8,128)(2,1)} collective-permute-done((bf16[384,768]{1,0:T(8,128)(2,1)S(1)}, bf16[384,768]{1,0:T(8,128)(2,1)}, u32[]{:S(2)}, u32[]{:S(2)}) %collective-permute-start.17) | collective-permute-done | bytes 589856 | tf_op jit(solution)/shard_map/ppermute | solution.py:22
  105.5 1.9 constant_dynamic-update-slice_fusion.8
  109.9 6.7 %add_convert_fusion = bf16[5,197,2304]{2,1,0:T(8,128)(2,1)S(1)} fusion(f32[2304]{0:T(1024)S(1)} %maximum_convert_fusion, bf16[768,2304]{1,0:T(8,128)(2,1)} %constant_dynamic-update-slice_fusion.18, bf16[5,197,768]{2,1,0:T(8,128)(2,1)S(1)} %copy-done.2, f32[768]{0:T(1024)S(1)} %reshape.369, f32[768]{0:T(1024)S(1)} %reshape.368, f32[5,197]{1,0:T(8,128)S(1)} %fusion.94, ...), kind=kOutput, calls=%fused_computation.23 | convolution fusion | flops 3494937600 | bytes 9614024 | tf_op jit(solution)/shard_map/bsd,de->bse/dot_general | solution.py:162
  118.6 3.8 copy.63
  122.4 2.2 copy.62
  124.6 2.6 copy.61
  127.2 4.7 multiply_reduce_fusion.1
  131.9 2.9 fusion.9
  136.3 3.0 fusion.61
  139.4 3.0 fusion.112
  142.9 2.4 constant_dynamic-update-slice_fusion.6
  145.3 10.8 %fusion.40 = f32[5,197,3072]{2,1,0:T(8,128)} fusion(bf16[768,3072]{1,0:T(8,128)(2,1)} %constant_dynamic-update-slice_fusion.6, f32[5,197,768]{2,1,0:T(8,128)S(1)} %get-tuple-element.51, f32[768]{0:T(1024)S(1)} %reshape.372, f32[768]{0:T(1024)S(1)} %reshape.371, f32[5,197]{1,0:T(8,128)S(1)} %fusion.95, f32[5,197]{1,0:T(8,128)S(1)} %broadcast_multiply_fusion), kind=kOutput, calls=%fused_computation.46 | convolution fusion | flops 4651595776 | bytes 19862216 | tf_op jit(solution)/shard_map/bsd,df->bsf/dot_general | solution.py:182
  156.1 12.3 %bitcast_convert_fusion = bf16[3072,768]{1,0:T(8,128)(2,1)} fusion(bf16[5,197,768]{2,1,0:T(8,128)(2,1)S(1)} %copy-done.9, f32[5]{0:T(128)S(1)} %compare_convert_fusion, f32[5,197,3072]{2,1,0:T(8,128)} %fusion.40, f32[3072]{0:T(1024)S(1)} %reshape.373), kind=kOutput, calls=%fused_computation.20 | convolution fusion | flops 4682700800 | bytes 18347540 | tf_op jit(solution)/shard_map/bsf,bsd->fd/dot_general | solution.py:194
  168.4 1.9 constant_dynamic-update-slice_fusion
  170.3 16.6 %convert_reduce_fusion = (f32[3072]{0:T(1024)S(1)}, bf16[5,197,3072]{2,1,0:T(8,128)(2,1)S(1)}) fusion(f32[5,197,3072]{2,1,0:T(8,128)} %fusion.40, f32[3072]{0:T(1024)S(1)} %reshape.373, bf16[3072,768]{1,0:T(8,128)(2,1)} %constant_dynamic-update-slice_fusion, bf16[5,197,768]{2,1,0:T(8,128)(2,1)S(1)} %copy-done.9, f32[5]{0:T(128)S(1)} %compare_convert_fusion), kind=kOutput, calls=%fused_computation.10 | convolution fusion | flops 4719675392 | bytes 24411668 | tf_op jit(solution)/shard_map/bsd,fd->bsf/dot_general | solution.py:196
  187.0 7.9 %multiply_reduce_fusion.2 = (f32[768]{0:T(1024)S(1)}, f32[5,197]{1,0:T(8,128)S(1)}, f32[768]{0:T(1024)S(1)}, f32[5,197,768]{2,1,0:T(8,128)S(1)}) fusion(f32[5,197,768]{2,1,0:T(8,128)S(1)} %get-tuple-element.51, f32[5,197]{1,0:T(8,128)S(1)} %fusion.95, f32[5,197]{1,0:T(8,128)S(1)} %broadcast_multiply_fusion, f32[768]{0:T(1024)S(1)} %reshape.371, ...), kind=kOutput, calls=%fused_computation.72 | convolution fusion | flops 4653862912 | bytes 16843308 | tf_op jit(solution)/shard_map/bsf,df->bsd/dot_general | solution.py:200
  194.9 7.7 %bitcast_convert_fusion.1 = bf16[768,3072]{1,0:T(8,128)(2,1)} fusion(bf16[5,197,3072]{2,1,0:T(8,128)(2,1)S(1)} %get-tuple-element.55, f32[5,197,768]{2,1,0:T(8,128)S(1)} %get-tuple-element.51, f32[768]{0:T(1024)S(1)} %reshape.372, f32[768]{0:T(1024)S(1)} %reshape.371, f32[5,197]{1,0:T(8,128)S(1)} %fusion.95, f32[5,197]{1,0:T(8,128)S(1)} %broadcast_multiply_fusion), kind=kOutput, calls=%fused_computation.21 | convolution fusion | flops 4653955072 | bytes 13810376 | tf_op jit(solution)/shard_map/bsd,bsf->df/dot_general | solution.py:198
  204.5 2.5 bitcast_convert_fusion.3
  207.0 3.8 convolution_convert_fusion
  210.9 4.0 copy.66
  214.8 8.6 %fusion.113 = f32[5,12,197,197]{2,3,1,0:T(8,128)} fusion(bf16[5,197,12,64]{1,3,2,0:T(8,128)(2,1)} %bitcast.168, bf16[5,197,12,64]{1,3,2,0:T(8,128)(2,1)} %bitcast.171), kind=kOutput, calls=%fused_computation.214 | convolution fusion | flops 298053120 | bytes 12340080 | tf_op jit(solution)/shard_map/bqhe,bkhe->bhqk/dot_general | solution.py:217
  223.4 8.1 %fusion.62 = bf16[5,12,64,197]{3,2,1,0:T(8,128)(2,1)} fusion(bf16[5,197,12,64]{1,3,2,0:T(8,128)(2,1)S(1)} %bitcast.169, f32[5,12,197,197]{2,3,1,0:T(8,128)} %copy-done, f32[5,12,197]{2,1,0:T(8,128)S(1)} %log_add_fusion), kind=kOutput, calls=%fused_computation.88 | convolution fusion | flops 305795232 | bytes 12387360 | tf_op jit(solution)/shard_map/bhqk,bqhe->bkhe/dot_general | solution.py:214
  231.5 20.3 %fusion.65 = bf16[5,12,64,197]{3,2,1,0:T(8,128)(2,1)} fusion(bf16[5,197,12,64]{1,3,2,0:T(8,128)(2,1)} %bitcast.173, f32[5,12,197,197]{2,3,1,0:T(8,128)} %fusion.113, f32[5,12,197,197]{2,3,1,0:T(8,128)} %copy-done, f32[5,12,197]{2,1,0:T(8,128)S(1)} %log_add_fusion), kind=kOutput, calls=%fused_computation.89 | convolution fusion | flops 319778464 | bytes 21701520 | tf_op jit(solution)/shard_map/bhqk,bkhe->bqhe/dot_general | solution.py:220
  251.8 19.2 %fusion.68 = bf16[5,12,64,197]{3,2,1,0:T(8,128)(2,1)} fusion(bf16[5,197,12,64]{1,3,2,0:T(8,128)(2,1)} %bitcast.175, f32[5,12,197,197]{2,3,1,0:T(8,128)} %fusion.113, f32[5,12,197,197]{2,3,1,0:T(8,128)} %copy-done, f32[5,12,197]{2,1,0:T(8,128)S(1)} %log_add_fusion), kind=kOutput, calls=%fused_computation.90 | convolution fusion | flops 319778464 | bytes 21701520 | tf_op jit(solution)/shard_map/bhqk,bqhe->bkhe/dot_general | solution.py:221
  271.0 3.8 copy.72
  274.8 3.8 copy.71
  278.6 3.8 copy.70
  282.5 9.4 %fusion.106 = (f32[768]{0:T(1024)S(1)}, f32[5,197]{1,0:T(8,128)S(1)}, f32[5,197,768]{2,1,0:T(8,128)}) fusion(f32[768]{0:T(1024)S(1)} %reshape.368, f32[5,197]{1,0:T(8,128)S(1)} %broadcast_multiply_fusion.1, bf16[5,197,768]{2,1,0:T(8,128)(2,1)} %param.16, bf16[768,2304]{1,0:T(8,128)(2,1)} %constant_dynamic-update-slice_fusion.18, ...), kind=kOutput, calls=%fused_computation.208 | convolution fusion | flops 3504013568 | bytes 12630728 | tf_op jit(solution)/shard_map/bse,de->bsd/dot_general | solution.py:234
  291.9 2.9 convert_reduce_fusion.1
  294.9 6.0 %bitcast_convert_fusion.2 = bf16[768,2304]{1,0:T(8,128)(2,1)} fusion(bf16[5,197,768]{2,1,0:T(8,128)(2,1)S(1)} %copy-done.3, f32[768]{0:T(1024)S(1)} %copy-done.27, f32[768]{0:T(1024)S(1)} %reshape.368, f32[5,197]{1,0:T(8,128)S(1)} %copy-done.22, f32[5,197]{1,0:T(8,128)S(1)} %broadcast_multiply_fusion.1, bf16[5,197,768]{2,1,0:T(8,128)(2,1)S(1)} %copy-done.11, ...), kind=kOutput, calls=%fused_computation.27 | convolution fusion | flops 3505784832 | bytes 9604808 | tf_op jit(solution)/shard_map/bsd,bse->de/dot_general | solution.py:230
  301.0 11.2 %multiply_convert_fusion.2 = bf16[5,197,768]{2,1,0:T(8,128)(2,1)} fusion(f32[5,197,768]{2,1,0:T(8,128)S(1)} %copy-done.8, bf16[3072,768]{1,0:T(8,128)(2,1)} %constant_dynamic-update-slice_fusion, f32[5]{0:T(128)S(1)} %compare_convert_fusion, f32[768]{0:T(1024)S(1)} %copy-done.25, f32[5,197,3072]{2,1,0:T(8,128)S(1)} %bitcast.217, f32[3072]{0:T(1024)S(1)} %reshape.373), kind=kOutput, calls=%fused_computation.79 | convolution fusion | flops 4681099264 | bytes 21376532 | tf_op jit(solution)/shard_map/bsf,fd->bsd/dot_general | solution.py:187
  314.8 3.9 fusion.56
  322.6 2.0 dynamic-slice_bitcast_fusion
  331.0 2.1 collective-permute-done.23
  333.1 2.6 collective-permute-start.24
  337.6 2.8 add_add_fusion.2
  344.5 2.1 collective-permute-done.35
  346.7 3.4 collective-permute-start.36
  350.7 2.4 collective-permute-done.36
  358.3 18.9 %collective-permute-done.26 = bf16[1,192,2304]{2,1,0:T(8,128)(2,1)S(1)} collective-permute-done((bf16[1,192,2304]{2,1,0:T(8,128)(2,1)S(1)}, bf16[1,192,2304]{2,1,0:T(8,128)(2,1)S(1)}, u32[]{:S(2)}, u32[]{:S(2)}) %collective-permute-start.26) | collective-permute-done | bytes 884768 | tf_op jit(solution)/shard_map/ppermute | solution.py:22
  381.0 4.8 collective-permute-done.27
  385.9 16.5 %collective-permute-done.47 = bf16[1,768,768]{2,1,0:T(8,128)(2,1)S(1)} collective-permute-done((bf16[1,768,768]{2,1,0:T(8,128)(2,1)S(1)}, bf16[1,768,768]{2,1,0:T(8,128)(2,1)S(1)}, u32[]{:S(2)}, u32[]{:S(2)}) %collective-permute-start.47) | collective-permute-done | bytes 1179680 | tf_op jit(solution)/shard_map/ppermute | solution.py:22
  403.5 18.9 %collective-permute-done.40 = bf16[1,192,3072]{2,1,0:T(8,128)(2,1)S(1)} collective-permute-done((bf16[1,192,3072]{2,1,0:T(8,128)(2,1)S(1)}, bf16[1,192,3072]{2,1,0:T(8,128)(2,1)S(1)}, u32[]{:S(2)}, u32[]{:S(2)}) %collective-permute-start.40) | collective-permute-done | bytes 1179680 | tf_op jit(solution)/shard_map/ppermute | solution.py:22
  425.9 7.0 %collective-permute-done.41 = bf16[96,3072]{1,0:T(8,128)(2,1)S(1)} collective-permute-done((bf16[96,3072]{1,0:T(8,128)(2,1)S(1)}, bf16[96,3072]{1,0:T(8,128)(2,1)S(1)}, u32[]{:S(2)}, u32[]{:S(2)}) %collective-permute-start.41) | collective-permute-done | bytes 589856 | tf_op jit(solution)/shard_map/ppermute | solution.py:22
  433.4 2.5 collective-permute-start.29
  435.9 7.8 %collective-permute-done.49 = bf16[192,768]{1,0:T(8,128)(2,1)S(1)} collective-permute-done((bf16[192,768]{1,0:T(8,128)(2,1)S(1)}, bf16[192,768]{1,0:T(8,128)(2,1)S(1)}, u32[]{:S(2)}, u32[]{:S(2)}) %collective-permute-start.49) | collective-permute-done | bytes 294944 | tf_op jit(solution)/shard_map/ppermute | solution.py:22
  443.9 3.3 collective-permute-done.42
  447.5 6.4 %collective-permute-start.30 = (bf16[48,2304]{1,0:T(8,128)(2,1)S(1)}, bf16[48,2304]{1,0:T(8,128)(2,1)S(1)}, u32[]{:S(2)}, u32[]{:S(2)}) collective-permute-start(bf16[48,2304]{1,0:T(8,128)(2,1)S(1)} %add_convert_fusion.8), channel_id=1, source_target_pairs={{0,8},{4,12},{8,0},{12,4},{16,24},{20,28},{24,16},{28,20},{1,9},{5... | collective-permute-start | bytes 663560 | tf_op jit(solution)/shard_map/ppermute | solution.py:22
  453.9 10.7 %collective-permute-done.50 = bf16[192,768]{1,0:T(8,128)(2,1)S(1)} collective-permute-done((bf16[192,768]{1,0:T(8,128)(2,1)S(1)}, bf16[192,768]{1,0:T(8,128)(2,1)S(1)}, u32[]{:S(2)}, u32[]{:S(2)}) %collective-permute-start.50) | collective-permute-done | bytes 294944 | tf_op jit(solution)/shard_map/ppermute | solution.py:22
  464.7 3.0 collective-permute-done.43
  469.4 4.6 collective-permute-done.51
  482.5 11.3 %collective-permute-done.52 = bf16[384,768]{1,0:T(8,128)(2,1)S(1)} collective-permute-done((bf16[384,768]{1,0:T(8,128)(2,1)S(1)}, bf16[384,768]{1,0:T(8,128)(2,1)S(1)}, u32[]{:S(2)}, u32[]{:S(2)}) %collective-permute-start.52) | collective-permute-done | bytes 589856 | tf_op jit(solution)/shard_map/ppermute | solution.py:22
  495.5 6.8 %collective-permute-done.45 = bf16[96,3072]{1,0:T(8,128)(2,1)S(1)} collective-permute-done((bf16[96,3072]{1,0:T(8,128)(2,1)S(1)}, bf16[96,3072]{1,0:T(8,128)(2,1)S(1)}, u32[]{:S(2)}, u32[]{:S(2)}) %collective-permute-start.45) | collective-permute-done | bytes 589856 | tf_op jit(solution)/shard_map/ppermute | solution.py:22
  (274 shorter events, 93.1 us)
Async XLA Ops:
  0.6 23.8 %copy-start.15 = (bf16[192,3072]{1,0:T(8,128)(2,1)S(1)}, bf16[192,3072]{1,0:T(8,128)(2,1)}, u32[]{:S(2)}) copy-start(bf16[192,3072]{1,0:T(8,128)(2,1)} %param.27) | copy-start | bytes 3538948
  0.7 22.9 %copy-start.2 = (bf16[5,197,768]{2,1,0:T(8,128)(2,1)S(1)}, bf16[5,197,768]{2,1,0:T(8,128)(2,1)}, u32[]{:S(2)}) copy-start(bf16[5,197,768]{2,1,0:T(8,128)(2,1)} %param.16) | copy-start | bytes 4538884
  0.7 40.8 %collective-permute-start.5 = (bf16[192,768]{1,0:T(8,128)(2,1)}, bf16[192,768]{1,0:T(8,128)(2,1)}, u32[]{:S(2)}, u32[]{:S(2)}) collective-permute-start(bf16[192,768]{1,0:T(8,128)(2,1)} %param.23), channel_id=1, source_target_pairs={{0,1},{1,0},{2,3},{3,2},{4,5},{5,4},{6,7},{7,6},{8,9},{9,8},{10,11... | collective-permute-start | bytes 884744 | tf_op jit(solution)/shard_map/ppermute | solution.py:22
  2.8 32.4 %collective-permute-start.6 = (bf16[96,768]{1,0:T(8,128)(2,1)}, bf16[96,768]{1,0:T(8,128)(2,1)S(1)}, u32[]{:S(2)}, u32[]{:S(2)}) collective-permute-start(bf16[96,768]{1,0:T(8,128)(2,1)} %dynamic-slice_bitcast_fusion.14), channel_id=1, source_target_pairs={{0,2},{1,3},{2,0},{3,1},{4,6},{5,7},{6,4},{7,5},{8,10},{9,11},{10,... | collective-permute-start | bytes 442376 | tf_op jit(solution)/shard_map/ppermute | solution.py:22
  5.5 43.8 %collective-permute-start = (bf16[192,2304]{1,0:T(8,128)(2,1)}, bf16[192,2304]{1,0:T(8,128)(2,1)}, u32[]{:S(2)}, u32[]{:S(2)}) collective-permute-start(bf16[192,2304]{1,0:T(8,128)(2,1)} %param.20), channel_id=1, source_target_pairs={{0,1},{1,0},{2,3},{3,2},{4,5},{5,4},{6,7},{7,6},{8,9},{9,8},{10,11... | collective-permute-start | bytes 2654216 | tf_op jit(solution)/shard_map/ppermute | solution.py:22
  7.3 19.0 %copy-start.19 = (bf16[192,768]{1,0:T(8,128)(2,1)S(1)}, bf16[192,768]{1,0:T(8,128)(2,1)}, u32[]{:S(2)}) copy-start(bf16[192,768]{1,0:T(8,128)(2,1)} %param.23) | copy-start | bytes 884740
  7.3 41.3 %collective-permute-start.1 = (bf16[96,2304]{1,0:T(8,128)(2,1)}, bf16[96,2304]{1,0:T(8,128)(2,1)}, u32[]{:S(2)}, u32[]{:S(2)}) collective-permute-start(bf16[96,2304]{1,0:T(8,128)(2,1)} %dynamic-slice_bitcast_fusion.9), channel_id=1, source_target_pairs={{0,2},{1,3},{2,0},{3,1},{4,6},{5,7},{6,4},{7,5},{8,10},{9,11},{10,... | collective-permute-start | bytes 1327112 | tf_op jit(solution)/shard_map/ppermute | solution.py:22
  7.6 68.5 %collective-permute-start.10 = (bf16[192,3072]{1,0:T(8,128)(2,1)}, bf16[192,3072]{1,0:T(8,128)(2,1)}, u32[]{:S(2)}, u32[]{:S(2)}) collective-permute-start(bf16[192,3072]{1,0:T(8,128)(2,1)} %param.27), channel_id=1, source_target_pairs={{0,1},{1,0},{2,3},{3,2},{4,5},{5,4},{6,7},{7,6},{8,9},{9,8},{10,11... | collective-permute-start | bytes 3538952 | tf_op jit(solution)/shard_map/ppermute | solution.py:22
  24.2 85.7 %copy-start.21 = (f32[5,197]{1,0:T(8,128)}, f32[5,197]{1,0:T(8,128)S(1)}, u32[]{:S(2)}) copy-start(f32[5,197]{1,0:T(8,128)S(1)} %fusion.94) | copy-start | bytes 11824
  35.3 6.2 %collective-permute-start.7 = (bf16[96,768]{1,0:T(8,128)(2,1)S(1)}, bf16[96,768]{1,0:T(8,128)(2,1)}, u32[]{:S(2)}, u32[]{:S(2)}) collective-permute-start(bf16[96,768]{1,0:T(8,128)(2,1)S(1)} %collective-permute-done.6), channel_id=1, source_target_pairs={{0,4},{4,0},{8,12},{12,8},{16,20},{20,16},{24,28},{28,24},{1,5},{5... | collective-permute-start | bytes 442376 | tf_op jit(solution)/shard_map/ppermute | solution.py:22
  37.1 72.8 %copy-start.26 = (f32[768]{0:T(1024)}, f32[768]{0:T(1024)S(1)}, u32[]{:S(2)}) copy-start(f32[768]{0:T(1024)S(1)} %reshape.369) | copy-start | bytes 9220
  41.5 4.4 collective-permute-start.8
  41.5 6.3 %collective-permute-start.9 = (bf16[96,768]{1,0:T(8,128)(2,1)}, bf16[96,768]{1,0:T(8,128)(2,1)S(1)}, u32[]{:S(2)}, u32[]{:S(2)}) collective-permute-start(bf16[96,768]{1,0:T(8,128)(2,1)} %collective-permute-done.7), channel_id=1, source_target_pairs={{0,1},{1,0},{2,3},{3,2},{4,5},{5,4},{6,7},{7,6},{8,9},{9,8},{10,11... | collective-permute-start | bytes 442376 | tf_op jit(solution)/shard_map/ppermute | solution.py:22
  45.9 16.2 %collective-permute-start.11 = (bf16[96,3072]{1,0:T(8,128)(2,1)S(1)}, bf16[96,3072]{1,0:T(8,128)(2,1)S(1)}, u32[]{:S(2)}, u32[]{:S(2)}) collective-permute-start(bf16[96,3072]{1,0:T(8,128)(2,1)S(1)} %copy-done.20), channel_id=1, source_target_pairs={{0,2},{1,3},{2,0},{3,1},{4,6},{5,7},{6,4},{7,5},{8,10},{9,11},{10,... | collective-permute-start | bytes 1769480 | tf_op jit(solution)/shard_map/ppermute | solution.py:22
  47.8 26.0 %collective-permute-start.16 = (bf16[384,768]{1,0:T(8,128)(2,1)S(1)}, bf16[384,768]{1,0:T(8,128)(2,1)S(1)}, u32[]{:S(2)}, u32[]{:S(2)}) collective-permute-start(bf16[384,768]{1,0:T(8,128)(2,1)S(1)} %dynamic-slice_bitcast_fusion.6), channel_id=1, source_target_pairs={{0,2},{1,3},{2,0},{3,1},{4,6},{5,7},{6,4},{7,5},{8,10},{9,11},{10,... | collective-permute-start | bytes 1769480 | tf_op jit(solution)/shard_map/ppermute | solution.py:22
  48.6 26.7 %collective-permute-start.3 = (bf16[96,2304]{1,0:T(8,128)(2,1)}, bf16[96,2304]{1,0:T(8,128)(2,1)S(1)}, u32[]{:S(2)}, u32[]{:S(2)}) collective-permute-start(bf16[96,2304]{1,0:T(8,128)(2,1)} %collective-permute-done.1), channel_id=1, source_target_pairs={{0,1},{1,0},{2,3},{3,2},{4,5},{5,4},{6,7},{7,6},{8,9},{9,8},{10,11... | collective-permute-start | bytes 1327112 | tf_op jit(solution)/shard_map/ppermute | solution.py:22
  49.3 12.8 %collective-permute-start.2 = (bf16[96,2304]{1,0:T(8,128)(2,1)}, bf16[96,2304]{1,0:T(8,128)(2,1)S(1)}, u32[]{:S(2)}, u32[]{:S(2)}) collective-permute-start(bf16[96,2304]{1,0:T(8,128)(2,1)} %collective-permute-done.1), channel_id=1, source_target_pairs={{0,4},{4,0},{8,12},{12,8},{16,20},{20,16},{24,28},{28,24},{1,5},{5... | collective-permute-start | bytes 1327112 | tf_op jit(solution)/shard_map/ppermute | solution.py:22
  62.1 38.9 %collective-permute-start.15 = (bf16[768,768]{1,0:T(8,128)(2,1)S(1)}, bf16[768,768]{1,0:T(8,128)(2,1)S(1)}, u32[]{:S(2)}, u32[]{:S(2)}) collective-permute-start(bf16[768,768]{1,0:T(8,128)(2,1)S(1)} %copy-done.16), channel_id=1, source_target_pairs={{0,1},{1,0},{2,3},{3,2},{4,5},{5,4},{6,7},{7,6},{8,9},{9,8},{10,11... | collective-permute-start | bytes 3538952 | tf_op jit(solution)/shard_map/ppermute | solution.py:22
  62.1 46.1 %collective-permute-start.13 = (bf16[96,3072]{1,0:T(8,128)(2,1)S(1)}, bf16[96,3072]{1,0:T(8,128)(2,1)S(1)}, u32[]{:S(2)}, u32[]{:S(2)}) collective-permute-start(bf16[96,3072]{1,0:T(8,128)(2,1)S(1)} %collective-permute-done.11), channel_id=1, source_target_pairs={{0,1},{1,0},{2,3},{3,2},{4,5},{5,4},{6,7},{7,6},{8,9},{9,8},{10,11... | collective-permute-start | bytes 1769480 | tf_op jit(solution)/shard_map/ppermute | solution.py:22
  73.9 16.4 %collective-permute-start.12 = (bf16[96,3072]{1,0:T(8,128)(2,1)S(1)}, bf16[96,3072]{1,0:T(8,128)(2,1)}, u32[]{:S(2)}, u32[]{:S(2)}) collective-permute-start(bf16[96,3072]{1,0:T(8,128)(2,1)S(1)} %collective-permute-done.11), channel_id=1, source_target_pairs={{0,4},{4,0},{8,12},{12,8},{16,20},{20,16},{24,28},{28,24},{1,5},{5... | collective-permute-start | bytes 1769480 | tf_op jit(solution)/shard_map/ppermute | solution.py:22
  75.3 32.1 %collective-permute-start.18 = (bf16[384,768]{1,0:T(8,128)(2,1)S(1)}, bf16[384,768]{1,0:T(8,128)(2,1)S(1)}, u32[]{:S(2)}, u32[]{:S(2)}) collective-permute-start(bf16[384,768]{1,0:T(8,128)(2,1)S(1)} %collective-permute-done.16), channel_id=1, source_target_pairs={{0,1},{1,0},{2,3},{3,2},{4,5},{5,4},{6,7},{7,6},{8,9},{9,8},{10,11... | collective-permute-start | bytes 1769480 | tf_op jit(solution)/shard_map/ppermute | solution.py:22
  76.1 24.9 %collective-permute-start.17 = (bf16[384,768]{1,0:T(8,128)(2,1)S(1)}, bf16[384,768]{1,0:T(8,128)(2,1)}, u32[]{:S(2)}, u32[]{:S(2)}) collective-permute-start(bf16[384,768]{1,0:T(8,128)(2,1)S(1)} %collective-permute-done.16), channel_id=1, source_target_pairs={{0,4},{4,0},{8,12},{12,8},{16,20},{20,16},{24,28},{28,24},{1,5},{5... | collective-permute-start | bytes 1769480 | tf_op jit(solution)/shard_map/ppermute | solution.py:22
  90.2 18.9 %collective-permute-start.4 = (bf16[96,2304]{1,0:T(8,128)(2,1)S(1)}, bf16[96,2304]{1,0:T(8,128)(2,1)S(1)}, u32[]{:S(2)}, u32[]{:S(2)}) collective-permute-start(bf16[96,2304]{1,0:T(8,128)(2,1)S(1)} %collective-permute-done.2), channel_id=1, source_target_pairs={{0,1},{1,0},{2,3},{3,2},{4,5},{5,4},{6,7},{7,6},{8,9},{9,8},{10,11... | collective-permute-start | bytes 1327112 | tf_op jit(solution)/shard_map/ppermute | solution.py:22
  101.0 41.9 %collective-permute-start.14 = (bf16[96,3072]{1,0:T(8,128)(2,1)}, bf16[96,3072]{1,0:T(8,128)(2,1)}, u32[]{:S(2)}, u32[]{:S(2)}) collective-permute-start(bf16[96,3072]{1,0:T(8,128)(2,1)} %collective-permute-done.12), channel_id=1, source_target_pairs={{0,1},{1,0},{2,3},{3,2},{4,5},{5,4},{6,7},{7,6},{8,9},{9,8},{10,11... | collective-permute-start | bytes 1769480 | tf_op jit(solution)/shard_map/ppermute | solution.py:22
  101.0 67.4 %collective-permute-start.19 = (bf16[384,768]{1,0:T(8,128)(2,1)}, bf16[384,768]{1,0:T(8,128)(2,1)}, u32[]{:S(2)}, u32[]{:S(2)}) collective-permute-start(bf16[384,768]{1,0:T(8,128)(2,1)} %collective-permute-done.17), channel_id=1, source_target_pairs={{0,1},{1,0},{2,3},{3,2},{4,5},{5,4},{6,7},{7,6},{8,9},{9,8},{10,11... | collective-permute-start | bytes 1769480 | tf_op jit(solution)/shard_map/ppermute | solution.py:22
  142.3 60.3 %copy-start.7 = (f32[5,197,768]{2,1,0:T(8,128)}, f32[5,197,768]{2,1,0:T(8,128)S(1)}, u32[]{:S(2)}) copy-start(f32[5,197,768]{2,1,0:T(8,128)S(1)} %get-tuple-element.51) | copy-start | bytes 9077764
  145.3 10.8 %copy-start.9 = (bf16[5,197,768]{2,1,0:T(8,128)(2,1)S(1)}, bf16[5,197,768]{2,1,0:T(8,128)(2,1)}, u32[]{:S(2)}) copy-start(bf16[5,197,768]{2,1,0:T(8,128)(2,1)} %param.31) | copy-start | bytes 4538884
  301.0 13.5 %copy-start.24 = (f32[5,197]{1,0:T(8,128)S(1)}, f32[5,197]{1,0:T(8,128)}, u32[]{:S(2)}) copy-start(f32[5,197]{1,0:T(8,128)} %copy-done.23) | copy-start | bytes 11824
  314.5 12.1 %collective-permute-start.32 = (bf16[2,192,768]{2,1,0:T(8,128)(2,1)}, bf16[2,192,768]{2,1,0:T(8,128)(2,1)}, u32[]{:S(2)}, u32[]{:S(2)}) collective-permute-start(bf16[2,192,768]{2,1,0:T(8,128)(2,1)} %dynamic-slice_bitcast_fusion.5), channel_id=1, source_target_pairs={{0,1},{1,0},{2,3},{3,2},{4,5},{5,4},{6,7},{7,6},{8,9},{9,8},{10,11... | collective-permute-start | bytes 1769480 | tf_op jit(solution)/shard_map/ppermute | solution.py:22
  318.9 2.4 collective-permute-start.20
  321.4 3.8 collective-permute-start.21
  324.6 31.3 %collective-permute-start.46 = (bf16[2,768,768]{2,1,0:T(8,128)(2,1)S(1)}, bf16[2,768,768]{2,1,0:T(8,128)(2,1)S(1)}, u32[]{:S(2)}, u32[]{:S(2)}) collective-permute-start(bf16[2,768,768]{2,1,0:T(8,128)(2,1)S(1)} %dynamic-slice_bitcast_fusion), channel_id=1, source_target_pairs={{0,1},{1,0},{2,3},{3,2},{4,5},{5,4},{6,7},{7,6},{8,9},{9,8},{10,11... | collective-permute-start | bytes 7077896 | tf_op jit(solution)/shard_map/ppermute | solution.py:22
  324.7 32.7 %collective-permute-start.39 = (bf16[2,192,3072]{2,1,0:T(8,128)(2,1)S(1)}, bf16[2,192,3072]{2,1,0:T(8,128)(2,1)S(1)}, u32[]{:S(2)}, u32[]{:S(2)}) collective-permute-start(bf16[2,192,3072]{2,1,0:T(8,128)(2,1)S(1)} %dynamic-slice_bitcast_fusion.1), channel_id=1, source_target_pairs={{0,1},{1,0},{2,3},{3,2},{4,5},{5,4},{6,7},{7,6},{8,9},{9,8},{10,11... | collective-permute-start | bytes 7077896 | tf_op jit(solution)/shard_map/ppermute | solution.py:22
  325.2 4.2 collective-permute-start.22
  326.6 11.0 %copy-start.10 = (bf16[5,197,768]{2,1,0:T(8,128)(2,1)S(1)}, bf16[5,197,768]{2,1,0:T(8,128)(2,1)}, u32[]{:S(2)}) copy-start(bf16[5,197,768]{2,1,0:T(8,128)(2,1)} %param.31) | copy-start | bytes 4538884
  328.0 8.8 %collective-permute-start.33 = (bf16[1,192,768]{2,1,0:T(8,128)(2,1)S(1)}, bf16[1,192,768]{2,1,0:T(8,128)(2,1)S(1)}, u32[]{:S(2)}, u32[]{:S(2)}) collective-permute-start(bf16[1,192,768]{2,1,0:T(8,128)(2,1)S(1)} %constant_dynamic-slice_fusion.2), channel_id=1, source_target_pairs={{0,2},{1,3},{2,0},{3,1},{4,6},{5,7},{6,4},{7,5},{8,10},{9,11},{10,... | collective-permute-start | bytes 884744 | tf_op jit(solution)/shard_map/ppermute | solution.py:22
  329.2 26.6 %slice-start = ((s8[4718592]{0:T(1024)(128)(4,1)}), s8[4194304]{0:T(1024)(128)(4,1)S(1)}, s32[]{:S(2)}) async-start(s8[4718592]{0:T(1024)(128)(4,1)} %bitcast.178), calls=%async_computation | async-start | bytes 8388608
  329.4 3.8 collective-permute-start.23
  331.0 23.0 %collective-permute-start.25 = (bf16[2,192,2304]{2,1,0:T(8,128)(2,1)S(1)}, bf16[2,192,2304]{2,1,0:T(8,128)(2,1)S(1)}, u32[]{:S(2)}, u32[]{:S(2)}) collective-permute-start(bf16[2,192,2304]{2,1,0:T(8,128)(2,1)S(1)} %dynamic-slice_bitcast_fusion.2), channel_id=1, source_target_pairs={{0,1},{1,0},{2,3},{3,2},{4,5},{5,4},{6,7},{7,6},{8,9},{9,8},{10,11... | collective-permute-start | bytes 5308424 | tf_op jit(solution)/shard_map/ppermute | solution.py:22
  333.1 7.2 %collective-permute-start.24 = (f32[1,18,128]{2,1,0:T(8,128)S(1)}, f32[1,18,128]{2,1,0:T(8,128)S(1)}, u32[]{:S(2)}, u32[]{:S(2)}) collective-permute-start(f32[1,18,128]{2,1,0:T(8,128)S(1)} %add.381), channel_id=1, source_target_pairs={{0,16},{4,20},{8,24},{12,28},{16,0},{20,4},{24,8},{28,12},{1,17},{... | collective-permute-start | bytes 27656 | tf_op jit(solution)/shard_map/ppermute | solution.py:22
  336.9 18.9 %slice-start.1 = ((s8[4718592]{0:T(1024)(128)(4,1)}), s8[524288]{0:T(1024)(128)(4,1)S(1)}, s32[]{:S(2)}) async-start(s8[4718592]{0:T(1024)(128)(4,1)} %bitcast.178), calls=%async_computation.1 | async-start | bytes 1048576
  336.9 5.2 %collective-permute-start.34 = (bf16[96,768]{1,0:T(8,128)(2,1)S(1)}, bf16[96,768]{1,0:T(8,128)(2,1)S(1)}, u32[]{:S(2)}, u32[]{:S(2)}) collective-permute-start(bf16[96,768]{1,0:T(8,128)(2,1)S(1)} %dynamic-slice_bitcast_fusion.13), channel_id=1, source_target_pairs={{0,4},{4,0},{8,12},{12,8},{16,20},{20,16},{24,28},{28,24},{1,5},{5... | collective-permute-start | bytes 442376 | tf_op jit(solution)/shard_map/ppermute | solution.py:22
  342.2 4.4 collective-permute-start.35
  346.7 6.4 %collective-permute-start.36 = (bf16[48,768]{1,0:T(8,128)(2,1)S(1)}, bf16[48,768]{1,0:T(8,128)(2,1)S(1)}, u32[]{:S(2)}, u32[]{:S(2)}) collective-permute-start(bf16[48,768]{1,0:T(8,128)(2,1)S(1)} %fusion.91), channel_id=1, source_target_pairs={{0,16},{4,20},{8,24},{12,28},{16,0},{20,4},{24,8},{28,12},{1,17},{... | collective-permute-start | bytes 221192 | tf_op jit(solution)/shard_map/ppermute | solution.py:22
  353.1 26.3 %collective-permute-start.37 = (bf16[48,768]{1,0:T(8,128)(2,1)S(1)}, bf16[48,768]{1,0:T(8,128)(2,1)S(1)}, u32[]{:S(2)}, u32[]{:S(2)}) collective-permute-start(bf16[48,768]{1,0:T(8,128)(2,1)S(1)} %add_convert_fusion.9), channel_id=1, source_target_pairs={{0,8},{4,12},{8,0},{12,4},{16,24},{20,28},{24,16},{28,20},{1,9},{5... | collective-permute-start | bytes 221192 | tf_op jit(solution)/shard_map/ppermute | solution.py:22
  354.5 22.7 %collective-permute-start.26 = (bf16[1,192,2304]{2,1,0:T(8,128)(2,1)S(1)}, bf16[1,192,2304]{2,1,0:T(8,128)(2,1)S(1)}, u32[]{:S(2)}, u32[]{:S(2)}) collective-permute-start(bf16[1,192,2304]{2,1,0:T(8,128)(2,1)S(1)} %constant_dynamic-slice_fusion.3), channel_id=1, source_target_pairs={{0,2},{1,3},{2,0},{3,1},{4,6},{5,7},{6,4},{7,5},{8,10},{9,11},{10,... | collective-permute-start | bytes 2654216 | tf_op jit(solution)/shard_map/ppermute | solution.py:22
  356.5 45.9 %collective-permute-start.47 = (bf16[1,768,768]{2,1,0:T(8,128)(2,1)S(1)}, bf16[1,768,768]{2,1,0:T(8,128)(2,1)S(1)}, u32[]{:S(2)}, u32[]{:S(2)}) collective-permute-start(bf16[1,768,768]{2,1,0:T(8,128)(2,1)S(1)} %constant_dynamic-slice_fusion), channel_id=1, source_target_pairs={{0,2},{1,3},{2,0},{3,1},{4,6},{5,7},{6,4},{7,5},{8,10},{9,11},{10,... | collective-permute-start | bytes 3538952 | tf_op jit(solution)/shard_map/ppermute | solution.py:22
  377.4 8.4 %collective-permute-start.27 = (bf16[96,2304]{1,0:T(8,128)(2,1)S(1)}, bf16[96,2304]{1,0:T(8,128)(2,1)S(1)}, u32[]{:S(2)}, u32[]{:S(2)}) collective-permute-start(bf16[96,2304]{1,0:T(8,128)(2,1)S(1)} %dynamic-slice_bitcast_fusion.8), channel_id=1, source_target_pairs={{0,4},{4,0},{8,12},{12,8},{16,20},{20,16},{24,28},{28,24},{1,5},{5... | collective-permute-start | bytes 1327112 | tf_op jit(solution)/shard_map/ppermute | solution.py:22
  378.2 44.1 %collective-permute-start.40 = (bf16[1,192,3072]{2,1,0:T(8,128)(2,1)S(1)}, bf16[1,192,3072]{2,1,0:T(8,128)(2,1)S(1)}, u32[]{:S(2)}, u32[]{:S(2)}) collective-permute-start(bf16[1,192,3072]{2,1,0:T(8,128)(2,1)S(1)} %constant_dynamic-slice_fusion.1), channel_id=1, source_target_pairs={{0,2},{1,3},{2,0},{3,1},{4,6},{5,7},{6,4},{7,5},{8,10},{9,11},{10,... | collective-permute-start | bytes 3538952 | tf_op jit(solution)/shard_map/ppermute | solution.py:22
  379.5 99.2 %collective-permute-start.38 = (bf16[96,768]{1,0:T(8,128)(2,1)S(1)}, bf16[96,768]{1,0:T(8,128)(2,1)S(1)}, u32[]{:S(2)}, u32[]{:S(2)}) collective-permute-start(bf16[96,768]{1,0:T(8,128)(2,1)S(1)} %maximum_select_fusion.7), channel_id=1, source_target_pairs={{0,4},{4,0},{8,12},{12,8},{16,20},{20,16},{24,28},{28,24},{1,5},{5... | collective-permute-start | bytes 442376 | tf_op jit(solution)/shard_map/ppermute | solution.py:22
  402.8 21.1 %collective-permute-start.48 = (bf16[384,768]{1,0:T(8,128)(2,1)S(1)}, bf16[384,768]{1,0:T(8,128)(2,1)S(1)}, u32[]{:S(2)}, u32[]{:S(2)}) collective-permute-start(bf16[384,768]{1,0:T(8,128)(2,1)S(1)} %dynamic-slice_bitcast_fusion.3), channel_id=1, source_target_pairs={{0,4},{4,0},{8,12},{12,8},{16,20},{20,16},{24,28},{28,24},{1,5},{5... | collective-permute-start | bytes 1769480 | tf_op jit(solution)/shard_map/ppermute | solution.py:22
  422.8 10.0 %collective-permute-start.41 = (bf16[96,3072]{1,0:T(8,128)(2,1)S(1)}, bf16[96,3072]{1,0:T(8,128)(2,1)S(1)}, u32[]{:S(2)}, u32[]{:S(2)}) collective-permute-start(bf16[96,3072]{1,0:T(8,128)(2,1)S(1)} %dynamic-slice_bitcast_fusion.4), channel_id=1, source_target_pairs={{0,4},{4,0},{8,12},{12,8},{16,20},{20,16},{24,28},{28,24},{1,5},{5... | collective-permute-start | bytes 1769480 | tf_op jit(solution)/shard_map/ppermute | solution.py:22
  423.5 9.8 %collective-permute-start.28 = (bf16[48,2304]{1,0:T(8,128)(2,1)S(1)}, bf16[48,2304]{1,0:T(8,128)(2,1)S(1)}, u32[]{:S(2)}, u32[]{:S(2)}) collective-permute-start(bf16[48,2304]{1,0:T(8,128)(2,1)S(1)} %dynamic-slice_bitcast_fusion.12), channel_id=1, source_target_pairs={{0,8},{4,12},{8,0},{12,4},{16,24},{20,28},{24,16},{28,20},{1,9},{5... | collective-permute-start | bytes 663560 | tf_op jit(solution)/shard_map/ppermute | solution.py:22
  424.1 19.6 %collective-permute-start.49 = (bf16[192,768]{1,0:T(8,128)(2,1)S(1)}, bf16[192,768]{1,0:T(8,128)(2,1)S(1)}, u32[]{:S(2)}, u32[]{:S(2)}) collective-permute-start(bf16[192,768]{1,0:T(8,128)(2,1)S(1)} %dynamic-slice_bitcast_fusion.10), channel_id=1, source_target_pairs={{0,8},{4,12},{8,0},{12,4},{16,24},{20,28},{24,16},{28,20},{1,9},{5... | collective-permute-start | bytes 884744 | tf_op jit(solution)/shard_map/ppermute | solution.py:22
  433.0 14.2 %collective-permute-start.42 = (bf16[48,3072]{1,0:T(8,128)(2,1)S(1)}, bf16[48,3072]{1,0:T(8,128)(2,1)S(1)}, u32[]{:S(2)}, u32[]{:S(2)}) collective-permute-start(bf16[48,3072]{1,0:T(8,128)(2,1)S(1)} %dynamic-slice_bitcast_fusion.11), channel_id=1, source_target_pairs={{0,8},{4,12},{8,0},{12,4},{16,24},{20,28},{24,16},{28,20},{1,9},{5... | collective-permute-start | bytes 884744 | tf_op jit(solution)/shard_map/ppermute | solution.py:22
  433.4 14.0 %collective-permute-start.29 = (bf16[48,2304]{1,0:T(8,128)(2,1)S(1)}, bf16[48,2304]{1,0:T(8,128)(2,1)S(1)}, u32[]{:S(2)}, u32[]{:S(2)}) collective-permute-start(bf16[48,2304]{1,0:T(8,128)(2,1)S(1)} %fusion.88), channel_id=1, source_target_pairs={{0,16},{4,20},{8,24},{12,28},{16,0},{20,4},{24,8},{28,12},{1,17},{... | collective-permute-start | bytes 663560 | tf_op jit(solution)/shard_map/ppermute | solution.py:22
  443.8 20.8 %collective-permute-start.50 = (bf16[192,768]{1,0:T(8,128)(2,1)S(1)}, bf16[192,768]{1,0:T(8,128)(2,1)S(1)}, u32[]{:S(2)}, u32[]{:S(2)}) collective-permute-start(bf16[192,768]{1,0:T(8,128)(2,1)S(1)} %fusion.86), channel_id=1, source_target_pairs={{0,16},{4,20},{8,24},{12,28},{16,0},{20,4},{24,8},{28,12},{1,17},{... | collective-permute-start | bytes 884744 | tf_op jit(solution)/shard_map/ppermute | solution.py:22
  447.3 20.5 %collective-permute-start.43 = (bf16[48,3072]{1,0:T(8,128)(2,1)S(1)}, bf16[48,3072]{1,0:T(8,128)(2,1)S(1)}, u32[]{:S(2)}, u32[]{:S(2)}) collective-permute-start(bf16[48,3072]{1,0:T(8,128)(2,1)S(1)} %fusion.87), channel_id=1, source_target_pairs={{0,16},{4,20},{8,24},{12,28},{16,0},{20,4},{24,8},{28,12},{1,17},{... | collective-permute-start | bytes 884744 | tf_op jit(solution)/shard_map/ppermute | solution.py:22
  447.5 20.5 %collective-permute-start.30 = (bf16[48,2304]{1,0:T(8,128)(2,1)S(1)}, bf16[48,2304]{1,0:T(8,128)(2,1)S(1)}, u32[]{:S(2)}, u32[]{:S(2)}) collective-permute-start(bf16[48,2304]{1,0:T(8,128)(2,1)S(1)} %add_convert_fusion.8), channel_id=1, source_target_pairs={{0,8},{4,12},{8,0},{12,4},{16,24},{20,28},{24,16},{28,20},{1,9},{5... | collective-permute-start | bytes 663560 | tf_op jit(solution)/shard_map/ppermute | solution.py:22
  464.7 9.4 %collective-permute-start.51 = (bf16[192,768]{1,0:T(8,128)(2,1)S(1)}, bf16[192,768]{1,0:T(8,128)(2,1)S(1)}, u32[]{:S(2)}, u32[]{:S(2)}) collective-permute-start(bf16[192,768]{1,0:T(8,128)(2,1)S(1)} %add_convert_fusion.5), channel_id=1, source_target_pairs={{0,8},{4,12},{8,0},{12,4},{16,24},{20,28},{24,16},{28,20},{1,9},{5... | collective-permute-start | bytes 884744 | tf_op jit(solution)/shard_map/ppermute | solution.py:22
  467.9 9.4 %collective-permute-start.44 = (bf16[48,3072]{1,0:T(8,128)(2,1)S(1)}, bf16[48,3072]{1,0:T(8,128)(2,1)S(1)}, u32[]{:S(2)}, u32[]{:S(2)}) collective-permute-start(bf16[48,3072]{1,0:T(8,128)(2,1)S(1)} %add_convert_fusion.6), channel_id=1, source_target_pairs={{0,8},{4,12},{8,0},{12,4},{16,24},{20,28},{24,16},{28,20},{1,9},{5... | collective-permute-start | bytes 884744 | tf_op jit(solution)/shard_map/ppermute | solution.py:22
  468.0 13.2 %collective-permute-start.31 = (bf16[96,2304]{1,0:T(8,128)(2,1)S(1)}, bf16[96,2304]{1,0:T(8,128)(2,1)S(1)}, u32[]{:S(2)}, u32[]{:S(2)}) collective-permute-start(bf16[96,2304]{1,0:T(8,128)(2,1)S(1)} %maximum_select_fusion.5), channel_id=1, source_target_pairs={{0,4},{4,0},{8,12},{12,8},{16,20},{20,16},{24,28},{28,24},{1,5},{5... | collective-permute-start | bytes 1327112 | tf_op jit(solution)/shard_map/ppermute | solution.py:22
  474.3 19.6 %collective-permute-start.52 = (bf16[384,768]{1,0:T(8,128)(2,1)S(1)}, bf16[384,768]{1,0:T(8,128)(2,1)S(1)}, u32[]{:S(2)}, u32[]{:S(2)}) collective-permute-start(bf16[384,768]{1,0:T(8,128)(2,1)S(1)} %maximum_select_fusion.4), channel_id=1, source_target_pairs={{0,4},{4,0},{8,12},{12,8},{16,20},{20,16},{24,28},{28,24},{1,5},{5... | collective-permute-start | bytes 1769480 | tf_op jit(solution)/shard_map/ppermute | solution.py:22
  477.4 24.9 %collective-permute-start.45 = (bf16[96,3072]{1,0:T(8,128)(2,1)S(1)}, bf16[96,3072]{1,0:T(8,128)(2,1)S(1)}, u32[]{:S(2)}, u32[]{:S(2)}) collective-permute-start(bf16[96,3072]{1,0:T(8,128)(2,1)S(1)} %maximum_select_fusion.3), channel_id=1, source_target_pairs={{0,4},{4,0},{8,12},{12,8},{16,20},{20,16},{24,28},{28,24},{1,5},{5... | collective-permute-start | bytes 1769480 | tf_op jit(solution)/shard_map/ppermute | solution.py:22
  (24 other events, 151.3 us)

commit v2 on v1

v2 whole, which is shorter than its diff:
```python
import functools

import jax
import jax.numpy as jnp
from jax import lax
from jax.experimental import pallas as pl
from jax.experimental.pallas import tpu as pltpu
from jax.sharding import PartitionSpec as P

HEADS = 12
F32 = jnp.float32
BF16 = jnp.bfloat16
GELU_A = 0.7978845608028654
GELU_B = 0.044715


def swap(field, axis, size, bit):
    return lax.ppermute(field, axis, [(at, at ^ bit) for at in range(size)])


def is_power(size):
    return size & (size - 1) == 0


def pick(field, at, axis):
    return lax.dynamic_index_in_dim(field, at, axis, keepdims=False)


def gather_pieces(shard, sizes):
    groups, replicas = sizes
    rows = shard.shape[0]
    if groups != 4 or replicas % 2 or rows % 32:
        return (lax.all_gather(shard, "group", axis=0, tiled=True),)
    half = lax.axis_index("replica") & 1
    first = swap(pick(shard.reshape(2, rows // 2, -1), half, 0), "group", 4, 2)
    near = swap(shard, "group", 4, 1)
    second = swap(first, "replica", replicas, 1)
    far_first = swap(first, "group", 4, 1)
    far_second = swap(second, "group", 4, 1)
    return (shard, near, first, second, far_first, far_second)


def place_pieces(rows, pieces, me, half):
    if pieces == 1:
        return [0]
    part = rows // 2
    return [
        me * rows,
        (me ^ 1) * rows,
        (me ^ 2) * rows + half * part,
        (me ^ 2) * rows + (1 - half) * part,
        (me ^ 3) * rows + half * part,
        (me ^ 3) * rows + (1 - half) * part,
    ]


def add_low(left, right, kind):
    return (left.astype(F32) + right.astype(F32)).astype(kind)


def reduce_shards(grad, sizes, halvings):
    groups, replicas = sizes
    rows = grad.shape[0] // groups
    kind = grad.dtype
    if not (is_power(groups) and is_power(replicas)):
        shard = lax.psum_scatter(grad, "group", scatter_dimension=0, tiled=True)
        return lax.psum(shard.astype(F32), "replica")
    me = lax.axis_index("group")
    other = lax.axis_index("replica")
    tail = grad.shape[1:]
    field = grad.reshape((groups, rows) + tail)
    bit = 1
    while bit < groups:
        side = (me // bit) & 1
        pairs = field.reshape((field.shape[0] // 2, 2, rows) + tail)
        came = swap(pick(pairs, 1 - side, 1), "group", groups, bit)
        field = add_low(pick(pairs, side, 1), came, kind)
        bit *= 2
    field = field[0]
    done = []
    bit = 1
    while bit < replicas:
        side = (other // bit) & 1
        if len(done) < halvings:
            pairs = field.reshape((2, field.shape[0] // 2) + tail)
            came = swap(pick(pairs, 1 - side, 0), "replica", replicas, bit)
            field = add_low(pick(pairs, side, 0), came, kind)
            done.append((bit, side))
        else:
            field = add_low(field, swap(field, "replica", replicas, bit), kind)
        bit *= 2
    for bit, side in reversed(done):
        came = swap(field, "replica", replicas, bit)
        field = jnp.where(
            side == 0, jnp.concatenate([field, came]), jnp.concatenate([came, field])
        )
    return field.astype(F32)


def dot(left, right):
    return lax.dot_general(left, right, (((1,), (0,)), ((), ())), preferred_element_type=F32)


def dot_nt(left, right):
    return lax.dot_general(left, right, (((1,), (1,)), ((), ())), preferred_element_type=F32)


def dot_tn(left, right):
    return lax.dot_general(left, right, (((0,), (0,)), ((), ())), preferred_element_type=F32)


def per_image(body, place, blocked, whole, weights, outs, sums, flops, after=()):
    slots = blocked[0].shape[0]
    counts = [len(pieces) for pieces in weights]
    rows_of = [pieces[0].shape[0] for pieces in weights]
    total = [rows * (4 if len(pieces) > 1 else 1) for rows, pieces in zip(rows_of, weights)]

    def kernel(*refs):
        refs = list(refs)

        def take(count):
            taken = refs[:count]
            del refs[:count]
            return taken

        (where,) = take(1)
        blocked_refs = take(len(blocked))
        whole_refs = take(len(whole))
        piece_refs = [take(count) for count in counts]
        take(len(after))
        out_refs = take(len(outs))
        sum_refs = take(len(sums))
        weight_refs = take(len(weights))
        at = pl.program_id(0)

        @pl.when(at == 0)
        def _():
            copies = []
            for index, pieces in enumerate(piece_refs):
                starts = place_pieces(rows_of[index], len(pieces), where[0], where[1])
                for spot, (piece, start) in enumerate(zip(pieces, starts)):
                    target = weight_refs[index].at[pl.ds(pl.multiple_of(start, 16), piece.shape[0])]
                    copies.append(pltpu.make_async_copy(piece, target, refs[0].at[index, spot]))
            for copy in copies:
                copy.start()
            for ref in sum_refs:
                ref[...] = jnp.zeros_like(ref)
            for copy in copies:
                copy.wait()

        body(at, where, blocked_refs, whole_refs, weight_refs, out_refs, sum_refs)

    in_specs = [pl.BlockSpec(memory_space=pltpu.SMEM)]
    for array in blocked:
        in_specs.append(pl.BlockSpec((1,) + array.shape[1:], lambda i: (i, 0, 0)))
    for array in whole:
        in_specs.append(pl.BlockSpec(array.shape, lambda i: (0, 0)))
    pieces = [piece for parts in weights for piece in parts]
    in_specs += [pl.BlockSpec(memory_space=pl.ANY)] * (len(pieces) + len(after))
    out_specs = [pl.BlockSpec((1, rows, columns), lambda i: (i, 0, 0)) for rows, columns, _ in outs]
    out_specs += [pl.BlockSpec((1, columns), lambda i: (0, 0)) for columns in sums]
    shapes = [jax.ShapeDtypeStruct((slots, rows, columns), kind) for rows, columns, kind in outs]
    shapes += [jax.ShapeDtypeStruct((1, columns), F32) for columns in sums]
    scratch = [
        pltpu.VMEM((rows, parts[0].shape[1]), BF16) for rows, parts in zip(total, weights)
    ]
    if weights:
        scratch.append(pltpu.SemaphoreType.DMA((len(weights), 6)))
    moved = sum(array.size * array.dtype.itemsize for array in list(blocked) + pieces)
    moved += sum(shape.size * shape.dtype.itemsize for shape in shapes)
    return pl.pallas_call(
        kernel,
        grid=(slots,),
        in_specs=in_specs,
        out_specs=out_specs,
        out_shape=shapes,
        scratch_shapes=scratch,
        compiler_params=pltpu.CompilerParams(
            dimension_semantics=("arbitrary",), vmem_limit_bytes=56 * 2**20
        ),
        cost_estimate=pl.CostEstimate(flops=flops, bytes_accessed=moved, transcendentals=0),
    )(place, *blocked, *whole, *pieces, *after)


def normed(field):
    centred = field - jnp.mean(field, -1, keepdims=True)
    scale = lax.rsqrt(jnp.mean(centred * centred, -1, keepdims=True) + 1e-06)
    return centred * scale, scale


def norm_back(grad, gain, hat, scale):
    inner = grad * gain
    mean = jnp.mean(inner, -1, keepdims=True)
    along = jnp.mean(inner * hat, -1, keepdims=True)
    return scale * (inner - mean - hat * along)


def column_sum(field):
    return jnp.sum(field.astype(F32), 0, keepdims=True)


def query_body(at, where, blocked, whole, weights, outs, sums):
    gain, shift, bias = whole
    hat, _ = normed(blocked[0][0].astype(F32))
    low = (hat * gain[...] + shift[...]).astype(BF16)
    outs[0][0] = low
    width = low.shape[1]
    for part in range(3):
        cut = slice(part * width, (part + 1) * width)
        outs[1][0, :, cut] = (dot(low, weights[0][:, cut]) + bias[:, cut]).astype(BF16)


def attend_body(length, at, where, blocked, whole, weights, outs, sums):
    packed, images = blocked
    bias, gain, shift = whole
    rows, width = images.shape[1:]
    lanes = 2 * width // HEADS
    factor = (width // HEADS) ** (-0.5)
    low_lane = lax.broadcasted_iota(jnp.int32, (rows, lanes), 1) < lanes // 2
    key_there = lax.broadcasted_iota(jnp.int32, (rows, rows), 1) < length
    for pair in range(HEADS // 2):
        start = pair * lanes
        query = packed[0, :, start : start + lanes] * jnp.asarray(factor, BF16)
        keys = packed[0, :, width + start : width + start + lanes]
        values = packed[0, :, 2 * width + start : 2 * width + start + lanes]
        both = []
        for side in range(2):
            mine = low_lane if side == 0 else jnp.logical_not(low_lane)
            scores = dot_nt(jnp.where(mine, query, jnp.zeros_like(query)), keys)
            scores = jnp.where(key_there, scores, -1e30)
            expo = jnp.exp(scores - jnp.max(scores, -1, keepdims=True))
            probs = expo * (1.0 / jnp.sum(expo, -1, keepdims=True))
            both.append(dot(probs.astype(BF16), values))
        outs[0][0, :, start : start + lanes] = jnp.where(low_lane, both[0], both[1]).astype(BF16)
    middle = images[0].astype(F32) + dot(outs[0][0], weights[0][...]) + bias[...]
    outs[1][0] = middle
    hat, _ = normed(middle)
    outs[2][0] = (hat * gain[...] + shift[...]).astype(BF16)


def up_body(at, where, blocked, whole, weights, outs, sums):
    low = blocked[0][0]
    inner = weights[0].shape[1]
    width = low.shape[1]
    for start in range(0, inner, width):
        cut = slice(start, start + width)
        pre = dot(low, weights[0][:, cut]) + whole[0][:, cut]
        square = pre * pre
        bend = jnp.tanh(pre * (GELU_A + (GELU_A * GELU_B) * square))
        half = 0.5 + 0.5 * bend
        outs[0][0, :, cut] = (pre * half).astype(BF16)
        slope = GELU_A + (3.0 * GELU_A * GELU_B) * square
        outs[1][0, :, cut] = (half + (0.5 * pre) * ((1.0 - bend * bend) * slope)).astype(BF16)


def back_body(at, where, blocked, whole, weights, outs, sums):
    cotangent, slope, middle = blocked
    (gain,) = whole
    w_down, w_up, w_out = weights
    grad_low = cotangent[0]
    width = grad_low.shape[1]
    inner = slope.shape[2]
    grad_two = None
    for start in range(0, inner, width):
        cut = slice(start, start + width)
        grad_pre = dot_nt(grad_low, w_down[cut, :]) * slope[0, :, cut].astype(F32)
        low = grad_pre.astype(BF16)
        outs[0][0, :, cut] = low
        sums[0][:, cut] += column_sum(low)
        part = dot_nt(low, w_up[:, cut])
        grad_two = part if grad_two is None else grad_two + part
    hat, scale = normed(middle[0])
    sums[1][...] += column_sum(grad_two * hat)
    sums[2][...] += column_sum(grad_two)
    sums[3][...] += column_sum(grad_low)
    grad_middle = grad_low.astype(F32) + norm_back(grad_two, gain[...], hat, scale)
    outs[1][0] = grad_middle
    low = grad_middle.astype(BF16)
    outs[2][0] = low
    sums[4][...] += column_sum(low)
    outs[3][0] = dot_nt(low, w_out[...]).astype(BF16)


def attend_back_body(length, at, where, blocked, whole, weights, outs, sums):
    packed, grads = blocked
    rows, width = grads.shape[1:]
    lanes = 2 * width // HEADS
    factor = (width // HEADS) ** (-0.5)
    low_lane = lax.broadcasted_iota(jnp.int32, (rows, lanes), 1) < lanes // 2
    key_there = lax.broadcasted_iota(jnp.int32, (rows, rows), 0) < length
    for pair in range(HEADS // 2):
        start = pair * lanes
        cuts = [slice(at * width + start, at * width + start + lanes) for at in range(3)]
        query, keys, values = (packed[0, :, cut] for cut in cuts)
        grad = grads[0, :, start : start + lanes]
        scaled = query * jnp.asarray(factor, BF16)
        results = []
        for side in range(2):
            mine = low_lane if side == 0 else jnp.logical_not(low_lane)
            scores = dot_nt(jnp.where(mine, keys, jnp.zeros_like(keys)), scaled)
            scores = jnp.where(key_there, scores, -1e30)
            expo = jnp.exp(scores - jnp.max(scores, 0, keepdims=True))
            probs = expo * (1.0 / jnp.sum(expo, 0, keepdims=True))
            grad_probs = dot_nt(jnp.where(mine, values, jnp.zeros_like(values)), grad)
            inner = jnp.sum(probs * grad_probs, 0, keepdims=True)
            grad_scores = (probs * (grad_probs - inner) * factor).astype(BF16)
            results.append(
                (
                    dot_tn(grad_scores, keys),
                    dot(grad_scores, query),
                    dot(probs.astype(BF16), grad),
                )
            )
        for cut, left, right in zip(cuts, results[0], results[1]):
            low = jnp.where(low_lane, left, right).astype(BF16)
            outs[0][0, :, cut] = low
            sums[0][:, cut] += column_sum(low)


def input_body(length, at, where, blocked, whole, weights, outs, sums):
    packed, images, grad_middle = blocked
    grad_one = dot_nt(packed[0], weights[0][...])
    hat, scale = normed(images[0].astype(F32))
    sums[0][...] += column_sum(grad_one * hat)
    sums[1][...] += column_sum(grad_one)
    result = grad_middle[0] + norm_back(grad_one, whole[0][...], hat, scale)
    outs[0][0] = result[:length]


def down_body(length, at, where, blocked, whole, weights, outs, sums):
    hidden, middle = blocked
    result = middle[0] + dot(hidden[0], weights[0][...]) + whole[0][...]
    live = jnp.where(at < where[2], 1.0, 0.0).astype(F32)
    outs[0][0] = (result * live)[:length].astype(BF16)


def on_device(
    sizes,
    images,
    counts,
    ln1_gain,
    ln1_shift,
    w_qkv,
    b_query,
    b_value,
    w_out,
    b_out,
    ln2_gain,
    ln2_shift,
    w_up,
    b_up,
    w_down,
    b_down,
    cotangent,
):
    slots, length, width = images.shape
    inner = w_up.shape[1]
    rows = -(-length // 16) * 16
    vectors = (ln1_gain, ln1_shift, b_query, b_value, b_out, ln2_gain, ln2_shift, b_down, b_up)
    gathered = lax.all_gather(jnp.concatenate(vectors), "group", axis=0, tiled=False)
    ends = [0]
    for vector in vectors:
        ends.append(ends[-1] + vector.shape[0])
    small = [
        gathered[:, at:end].reshape(1, -1).astype(F32) for at, end in zip(ends, ends[1:])
    ]
    gain_one, shift_one, bias_query, bias_value, bias_out, gain_two, shift_two, bias_down, bias_up = small
    bias_cat = jnp.concatenate([bias_query, jnp.zeros_like(bias_query), bias_value], 1)
    w_qkv = gather_pieces(w_qkv, sizes)
    w_out = gather_pieces(w_out, sizes)
    w_up = gather_pieces(w_up, sizes)
    w_down = gather_pieces(w_down, sizes)
    place = jnp.stack(
        [lax.axis_index("group"), lax.axis_index("replica") & 1, counts[0], counts[0]]
    ).astype(jnp.int32)
    live = (jnp.arange(slots, dtype=jnp.int32) < counts[0]).astype(BF16)[:, None, None]
    fill = ((0, 0), (0, rows - length), (0, 0))
    images = jnp.pad(images, fill)
    cotangent = jnp.pad(cotangent * live, fill)
    tokens = slots * rows
    unit = 2 * tokens * width * width

    low_one, packed = per_image(
        query_body, place, [images], [gain_one, shift_one, bias_cat], [w_qkv],
        [(rows, width, BF16), (rows, 3 * width, BF16)], [], 3 * unit,
    )
    attended, middle, low_two = per_image(
        functools.partial(attend_body, length), place, [packed, images],
        [bias_out, gain_two, shift_two], [w_out],
        [(rows, width, BF16), (rows, width, F32), (rows, width, BF16)], [], 4 * unit,
    )
    hidden, slope = per_image(
        up_body, place, [low_two], [bias_up], [w_up],
        [(rows, inner, BF16), (rows, inner, BF16)], [], 6 * unit,
    )

    def outer(left, right):
        left = left.reshape(tokens, -1)
        right = right.reshape(tokens, -1)
        return dot_tn(left, right).astype(BF16)

    grad_down = outer(hidden, cotangent)
    grad_pre, grad_middle, grad_branch, grad_att, grad_bup, grad_gain_two, grad_shift_two, grad_bdown, grad_bout = per_image(
        back_body, place, [cotangent, slope, middle], [gain_two], [w_down, w_up, w_out],
        [(rows, inner, BF16), (rows, width, F32), (rows, width, BF16), (rows, width, BF16)],
        [inner, width, width, width, width], 10 * unit,
    )
    grad_up = outer(low_two, grad_pre)
    grad_proj_out = outer(attended, grad_branch)
    grad_packed, packed_sums = per_image(
        functools.partial(attend_back_body, length), place, [packed, grad_att], [], [],
        [(rows, 3 * width, BF16)], [3 * width], 8 * unit,
    )
    grad_qkv = outer(low_one, grad_packed)
    input_grad, grad_gain_one, grad_shift_one = per_image(
        functools.partial(input_body, length), place, [grad_packed, images, grad_middle],
        [gain_one], [w_qkv], [(length, width, F32)], [width, width], 4 * unit,
    )
    (outputs,) = per_image(
        functools.partial(down_body, length), place, [hidden, middle], [bias_down], [w_down],
        [(length, width, BF16)], [], 5 * unit,
    )
    big = [
        reduce_shards(grad, sizes, 2)
        for grad in (grad_down, grad_up, grad_proj_out, grad_qkv)
    ]
    parts = (
        grad_gain_one,
        grad_shift_one,
        packed_sums[:, :width],
        packed_sums[:, 2 * width :],
        grad_bout,
        grad_gain_two,
        grad_shift_two,
        grad_bdown,
        grad_bup,
    )
    joined = jnp.concatenate([part.reshape(sizes[0], -1) for part in parts], 1)
    little = reduce_shards(joined.reshape(sizes[0], -1, 128), sizes, 0).reshape(-1)
    sums = [little[at:end] for at, end in zip(ends, ends[1:])]
    return (
        outputs,
        input_grad,
        sums[0],
        sums[1],
        big[3],
        sums[2],
        sums[3],
        big[2],
        sums[4],
        sums[5],
        sums[6],
        big[1],
        sums[8],
        big[0],
        sums[7],
    )


def solution(mesh):
    sizes = (mesh.shape["group"], mesh.shape["replica"])
    line = P("group")
    grid = P("group", None)
    field = P(("replica", "group"), None, None)
    return jax.shard_map(
        functools.partial(on_device, sizes),
        mesh=mesh,
        in_specs=(
            field, P(("replica", "group")), line, line, grid, line, line, grid, line, line, line,
            grid, line, grid, line, field,
        ),
        out_specs=(
            field, field, line, line, grid, line, line, grid, line, line, line, grid, line, grid,
            line,
        ),
        check_vma=False,
    )
```

time: 510 us -> 410 us (0.80)
  matrix products: 162 us -> 24.7 us
  Pallas kernels: 0 us -> 118 us
  local copies, waits for them, and re-layouts: 87.7 us -> 25.8 us
  waiting for transfers between devices: 165 us -> 134 us
  blocking collectives: 7.25 us -> 29.8 us
  other arithmetic: 28.4 us -> 19.2 us
    dot_general x18 -> x4, matrix products: 162 us -> 24.7 us  [dot_tn(): lax.dot_general(left, right, (((0,), (0,)), ((), ())), preferred_element_...]
    pallas_call x0 -> x7, Pallas kernels: none -> 118 us  [per_image(): pl.pallas_call(kernel, grid=(slots,), in_specs=in_specs, out_specs=out_sp...]
    ppermute x53, waiting for transfers between devices: 165 us -> 134 us  [swap(): return lax.ppermute(field, axis, [(at, at ^ bit) for at in range(size)])]
    dynamic_update_slice x24 -> x0, local copies, waits for them, and re-layouts: 30.7 us -> none  [put(): lax.dynamic_update_slice(whole, part, (owner * rows + at * (rows // 2), 0))]
    all_gather x1, blocking collectives: 7.25 us -> 29.8 us  [on_device(): lax.all_gather(jnp.concatenate(vectors), 'group', axis=0, tiled=False)]
    reduce_sum x8 -> x0, other arithmetic: 14.4 us -> none  [the longest x1 3.95 us: layer_norm(): return centred * lax.rsqrt(spread + 1e-06) * gain + shift]
    reshape x3 -> x0, local copies, waits for them, and re-layouts: 11.5 us -> none  [the longest x1 3.82 us: on_device(): grad_value.reshape(slot_count, length, width)]
    slice x5 -> x1, local copies, waits for them, and re-layouts: 10.5 us -> 0.72 us  [on_device(): packed_sums[:, 2 * width:]]
  transfers between devices with their start and end apart: 53 -> 53, of which waited for: 24 -> 20; matrix products, arithmetic and copies ran while one was open for 26% -> 14% of each run, Pallas kernels for 0% -> 13%
where the time goes in v2:
time: 410 us; the launch traced here: 407 us
  waiting for transfers between devices  134 us (33%)
  Pallas kernels  118 us (29%)
  starting transfers between devices  51.9 us (13%)
  blocking collectives  29.8 us (7%)
  local copies, waits for them, and re-layouts  25.8 us (6%)
  matrix products  24.7 us (6%)
  other arithmetic  19.2 us (5%)
    ppermute x53, waiting for transfers between devices, swap(): return lax.ppermute(field, axis, [(at, at ^ bit) for at in range(size)])  134 us
    pallas_call x7, Pallas kernels, per_image(): pl.pallas_call(kernel, grid=(slots,), in_specs=in_specs, out_specs=out_sp...  118 us
    ppermute x53, starting transfers between devices, swap(): return lax.ppermute(field, axis, [(at, at ^ bit) for at in range(size)])  51.9 us
    all_gather x1, blocking collectives, on_device(): lax.all_gather(jnp.concatenate(vectors), 'group', axis=0, tiled=False)  29.8 us
    dot_general x4, matrix products, dot_tn(): lax.dot_general(left, right, (((0,), (0,)), ((), ())), preferred_element_...  24.7 us
    squeeze x22, local copies, waits for them, and re-layouts, pick(): return lax.dynamic_index_in_dim(field, at, axis, keepdims=False)  10.6 us
    convert_element_type x20, other arithmetic, add_low(): return (left.astype(F32) + right.astype(F32)).astype(kind)  9.73 us
  transfers between devices with their start and end apart: 53, of which 20 were waited for; matrix products, arithmetic and copies ran while one was open for 14% of the time, Pallas kernels for 13%

profile of v2, /device:TPU:0, one launch (start us, length us, event | category | flops | bytes accessed | tf_op | source)
XLA Modules:
  0.0 406.8 jit_solution(2922711896050237055)
XLA Ops:
  1.8 3.0 collective-permute-start.6
  5.9 1.9 dynamic-slice_bitcast_fusion.7
  7.8 2.0 collective-permute-start.11
  11.7 1.9 collective-permute-start.7
  14.7 29.8 %all-gather.1 = bf16[4,1,2304]{2,1,0:T(2,128)(2,1)S(1)} all-gather(bf16[1,1,2304]{2,1,0:T(2,128)(2,1)S(1)} %reshape.330), channel_id=2, replica_groups=mesh['replica'=8,'group'=4] {'group'}, dimensions={0}, use_global_device_ids=true | all-gather | bytes 23040 | tf_op jit(solution)/shard_map/all_gather | solution.py:360
  45.1 1.7 collective-permute-start.2
  47.8 10.6 %collective-permute-done.2.refs_8_ = bf16[96,2304]{1,0:T(8,128)(2,1)} collective-permute-done((bf16[96,2304]{1,0:T(8,128)(2,1)}, bf16[96,2304]{1,0:T(8,128)(2,1)}, u32[]{:S(2)}, u32[]{:S(2)}) %collective-permute-start.2) | collective-permute-done | bytes 442400 | tf_op jit(solution)/shard_map/ppermute | solution.py:18
  63.8 1.3 pad.7.refs_1_.refs_2_
  65.0 1.3 pad.8.refs_1_
  67.5 2.9 collective-permute-done.12.refs_6_.refs_14_
  70.4 1.7 collective-permute-start.17
  72.2 10.2 %shard_map.271 = (bf16[5,208,768]{2,1,0:T(8,128)(2,1)}, bf16[5,208,2304]{2,1,0:T(8,128)(2,1)}) custom-call(s32[4]{0:T(128)} %pad_add_fusion.refs_0_, bf16[5,208,768]{2,1,0:T(8,128)(2,1)} %pad.7.refs_1_.refs_2_, f32[1,768]{1,0:T(1,128)} %reshape.308.refs_2_.refs_4_, f32[1,768]{1,0:T(1,128)} %reshape.309.refs_3_, f32[1,2304]{1,0:T(1,128)} %fusion.16.refs_4_, ...), custom_call_target="tpu_custom_call" | custom-call | flops 3680501760 | bytes 11526144 | tf_op jit(solution)/shard_map/pallas_call | solution.py:171
  83.0 15.3 %shard_map.272 = (bf16[5,208,768]{2,1,0:T(8,128)(2,1)}, f32[5,208,768]{2,1,0:T(8,128)}, bf16[5,208,768]{2,1,0:T(8,128)(2,1)}) custom-call(s32[4]{0:T(128)} %pad_add_fusion.refs_0_, bf16[5,208,2304]{2,1,0:T(8,128)(2,1)} %get-tuple-element.36.refs_1_, bf16[5,208,768]{2,1,0:T(8,128)(2,1)} %pad.7.refs_1_.refs_2_, f32[1,768]{1,0:T(1,128)} %reshape.312.refs_3_, ...), custom_call_target="tpu_custom_call" | custom-call | flops 4907335680 | bytes 13959168 | tf_op jit(solution)/shard_map/pallas_call | solution.py:171
  99.9 16.9 %shard_map.273 = (bf16[5,208,3072]{2,1,0:T(8,128)(2,1)}, bf16[5,208,3072]{2,1,0:T(8,128)(2,1)}) custom-call(s32[4]{0:T(128)} %pad_add_fusion.refs_0_, bf16[5,208,768]{2,1,0:T(8,128)(2,1)} %get-tuple-element.37.refs_1_, f32[1,3072]{1,0:T(1,128)} %bitcast.154, bf16[192,3072]{1,0:T(8,128)(2,1)} %refs_11_.1, ...), custom_call_target="tpu_custom_call" | custom-call | flops 7361003520 | bytes 19095552 | tf_op jit(solution)/shard_map/pallas_call | solution.py:171
  116.8 11.0 %bitcast_convert_fusion = bf16[3072,768]{1,0:T(8,128)(2,1)} fusion(bf16[5,208,3072]{2,1,0:T(8,128)(2,1)} %get-tuple-element.38.refs_1_, bf16[5,197,768]{2,1,0:T(8,128)(2,1)S(1)} %broadcast_multiply_fusion), kind=kOutput, calls=%fused_computation | convolution fusion | flops 4909694976 | bytes 12621312 | tf_op jit(solution)/shard_map/dot_general | solution.py:109
  129.1 25.7 %shard_map.275 = (bf16[5,208,3072]{2,1,0:T(8,128)(2,1)}, f32[5,208,768]{2,1,0:T(8,128)}, bf16[5,208,768]{2,1,0:T(8,128)(2,1)}, bf16[5,208,768]{2,1,0:T(8,128)(2,...) custom-call(s32[4]{0:T(128)} %pad_add_fusion.refs_0_, ...), custom_call_target="tpu_custom_call" | custom-call | flops 12268339200 | bytes 34603008 | tf_op jit(solution)/shard_map/pallas_call | solution.py:171
  154.8 25.7 %shard_map.276 = (bf16[5,208,2304]{2,1,0:T(8,128)(2,1)}, f32[1,2304]{1,0:T(1,128)}) custom-call(s32[4]{0:T(128)} %pad_add_fusion.refs_0_, bf16[5,208,2304]{2,1,0:T(8,128)(2,1)} %get-tuple-element.36.refs_1_, bf16[5,208,768]{2,1,0:T(8,128)(2,1)} %get-tuple-element.41.refs_2_), custom_call_target="tpu_custom_call" | custom-call | flops 9814671360 | bytes 11191296 | tf_op jit(solution)/shard_map/pallas_call | solution.py:171
  181.4 12.9 %shard_map.277 = (f32[5,197,768]{2,1,0:T(8,128)}, f32[1,768]{1,0:T(1,128)}, f32[1,768]{1,0:T(1,128)}) custom-call(s32[4]{0:T(128)} %pad_add_fusion.refs_0_, bf16[5,208,2304]{2,1,0:T(8,128)(2,1)} %get-tuple-element.42.refs_1_, bf16[5,208,768]{2,1,0:T(8,128)(2,1)} %pad.7.refs_1_.refs_2_, f32[5,208,768]{2,1,0:T(8,128)} %get-tuple-element.43.refs_3_, ...), custom_call_target="tpu_custom_call" | custom-call | flops 4907335680 | bytes 16155648 | tf_op jit(solution)/shard_map/pallas_call | solution.py:171
  198.1 1.8 bitcast_convert_fusion.3
  201.0 5.0 %bitcast_convert_fusion.2 = bf16[768,2304]{1,0:T(8,128)(2,1)S(1)} fusion(bf16[5,208,768]{2,1,0:T(8,128)(2,1)S(1)} %copy-done.29, bf16[5,208,2304]{2,1,0:T(8,128)(2,1)S(1)} %copy-done.26), kind=kOutput, calls=%fused_computation.2 | convolution fusion | flops 3682271232 | bytes 9928704 | tf_op jit(solution)/shard_map/dot_general | solution.py:109
  206.0 1.3 dynamic-slice_bitcast_fusion.2
  207.6 1.6 collective-permute-start.21
  209.2 1.6 dynamic-slice_bitcast_fusion
  211.7 6.9 %bitcast_convert_fusion.1 = bf16[768,3072]{1,0:T(8,128)(2,1)S(1)} fusion(bf16[5,208,768]{2,1,0:T(8,128)(2,1)S(1)} %copy-done.30, bf16[5,208,3072]{2,1,0:T(8,128)(2,1)S(1)} %bitcast.156), kind=kOutput, calls=%fused_computation.1 | convolution fusion | flops 4909694976 | bytes 12705792 | tf_op jit(solution)/shard_map/dot_general | solution.py:109
  218.6 1.9 collective-permute-start.23
  220.7 1.6 collective-permute-start.33
  222.3 1.6 dynamic-slice_bitcast_fusion.1
  223.9 2.6 collective-permute-start.24
  226.5 2.5 collective-permute-done.33
  230.5 1.5 collective-permute-start.34
  232.0 11.5 %shard_map.274 = bf16[5,197,768]{2,1,0:T(8,128)(2,1)} custom-call(s32[4]{0:T(128)} %pad_add_fusion.refs_0_, bf16[5,208,3072]{2,1,0:T(8,128)(2,1)} %get-tuple-element.38.refs_1_, f32[5,208,768]{2,1,0:T(8,128)} %get-tuple-element.39.refs_2_.refs_3_, f32[1,768]{1,0:T(1,128)} %reshape.316.refs_3_, bf16[768,768]{1,0:T(8,128)(2,1)} %refs_5_.4, ...), custom_call_target="tpu_custom_call" | custom-call | flops 6134169600 | bytes 15816192 | tf_op jit(solution)/shard_map/pallas_call | solution.py:171
  245.8 3.3 collective-permute-done.35
  249.0 2.7 collective-permute-start.36
  252.3 2.8 collective-permute-done.36
  255.2 1.9 fusion.2
  257.2 1.5 collective-permute-start.26
  258.7 2.2 fusion
  262.1 2.6 fusion.1
  264.7 15.2 %collective-permute-done.26 = bf16[1,192,2304]{2,1,0:T(8,128)(2,1)S(1)} collective-permute-done((bf16[1,192,2304]{2,1,0:T(8,128)(2,1)S(1)}, bf16[1,192,2304]{2,1,0:T(8,128)(2,1)S(1)}, u32[]{:S(2)}, u32[]{:S(2)}) %collective-permute-start.26) | collective-permute-done | bytes 884768 | tf_op jit(solution)/shard_map/ppermute | solution.py:18
  280.8 1.5 collective-permute-start.40
  282.4 1.6 collective-permute-start.38
  283.9 4.6 %collective-permute-done.27 = bf16[96,2304]{1,0:T(8,128)(2,1)S(1)} collective-permute-done((bf16[96,2304]{1,0:T(8,128)(2,1)S(1)}, bf16[96,2304]{1,0:T(8,128)(2,1)S(1)}, u32[]{:S(2)}, u32[]{:S(2)}) %collective-permute-start.27) | collective-permute-done | bytes 442400 | tf_op jit(solution)/shard_map/ppermute | solution.py:18
  288.6 16.5 %collective-permute-done.47 = bf16[1,768,768]{2,1,0:T(8,128)(2,1)S(1)} collective-permute-done((bf16[1,768,768]{2,1,0:T(8,128)(2,1)S(1)}, bf16[1,768,768]{2,1,0:T(8,128)(2,1)S(1)}, u32[]{:S(2)}, u32[]{:S(2)}) %collective-permute-start.47) | collective-permute-done | bytes 1179680 | tf_op jit(solution)/shard_map/ppermute | solution.py:18
  306.2 19.0 %collective-permute-done.40 = bf16[1,192,3072]{2,1,0:T(8,128)(2,1)S(1)} collective-permute-done((bf16[1,192,3072]{2,1,0:T(8,128)(2,1)S(1)}, bf16[1,192,3072]{2,1,0:T(8,128)(2,1)S(1)}, u32[]{:S(2)}, u32[]{:S(2)}) %collective-permute-start.40) | collective-permute-done | bytes 1179680 | tf_op jit(solution)/shard_map/ppermute | solution.py:18
  326.4 1.8 collective-permute-start.28
  328.7 7.0 %collective-permute-done.41 = bf16[96,3072]{1,0:T(8,128)(2,1)S(1)} collective-permute-done((bf16[96,3072]{1,0:T(8,128)(2,1)S(1)}, bf16[96,3072]{1,0:T(8,128)(2,1)S(1)}, u32[]{:S(2)}, u32[]{:S(2)}) %collective-permute-start.41) | collective-permute-done | bytes 589856 | tf_op jit(solution)/shard_map/ppermute | solution.py:18
  335.9 1.6 collective-permute-start.42
  337.6 2.0 collective-permute-start.29
  339.6 6.3 %collective-permute-done.49 = bf16[192,768]{1,0:T(8,128)(2,1)S(1)} collective-permute-done((bf16[192,768]{1,0:T(8,128)(2,1)S(1)}, bf16[192,768]{1,0:T(8,128)(2,1)S(1)}, u32[]{:S(2)}, u32[]{:S(2)}) %collective-permute-start.49) | collective-permute-done | bytes 294944 | tf_op jit(solution)/shard_map/ppermute | solution.py:18
  346.0 1.7 collective-permute-start.50
  347.8 2.0 collective-permute-done.42
  349.8 1.4 collective-permute-start.43
  351.3 2.5 collective-permute-start.30
  353.8 13.1 %collective-permute-done.50 = bf16[192,768]{1,0:T(8,128)(2,1)S(1)} collective-permute-done((bf16[192,768]{1,0:T(8,128)(2,1)S(1)}, bf16[192,768]{1,0:T(8,128)(2,1)S(1)}, u32[]{:S(2)}, u32[]{:S(2)}) %collective-permute-start.50) | collective-permute-done | bytes 294944 | tf_op jit(solution)/shard_map/ppermute | solution.py:18
  367.1 3.0 collective-permute-done.43
  370.4 1.8 collective-permute-start.31
  372.2 4.2 %collective-permute-done.51 = bf16[192,768]{1,0:T(8,128)(2,1)S(1)} collective-permute-done((bf16[192,768]{1,0:T(8,128)(2,1)S(1)}, bf16[192,768]{1,0:T(8,128)(2,1)S(1)}, u32[]{:S(2)}, u32[]{:S(2)}) %collective-permute-start.51) | collective-permute-done | bytes 294944 | tf_op jit(solution)/shard_map/ppermute | solution.py:18
  376.6 1.8 collective-permute-start.52
  379.7 1.8 collective-permute-start.45
  383.6 1.3 fusion.8
  384.9 11.3 %collective-permute-done.52 = bf16[384,768]{1,0:T(8,128)(2,1)S(1)} collective-permute-done((bf16[384,768]{1,0:T(8,128)(2,1)S(1)}, bf16[384,768]{1,0:T(8,128)(2,1)S(1)}, u32[]{:S(2)}, u32[]{:S(2)}) %collective-permute-start.52) | collective-permute-done | bytes 589856 | tf_op jit(solution)/shard_map/ppermute | solution.py:18
  396.2 1.6 fusion.4
  397.8 6.9 %collective-permute-done.45 = bf16[96,3072]{1,0:T(8,128)(2,1)S(1)} collective-permute-done((bf16[96,3072]{1,0:T(8,128)(2,1)S(1)}, bf16[96,3072]{1,0:T(8,128)(2,1)S(1)}, u32[]{:S(2)}, u32[]{:S(2)}) %collective-permute-start.45) | collective-permute-done | bytes 589856 | tf_op jit(solution)/shard_map/ppermute | solution.py:18
  404.7 1.7 fusion.3
  (230 shorter events, 36.7 us)
Async XLA Ops:
  0.7 13.0 %copy-start.1 = (bf16[5,197,768]{2,1,0:T(8,128)(2,1)S(1)}, bf16[5,197,768]{2,1,0:T(8,128)(2,1)}, u32[]{:S(2)}) copy-start(bf16[5,197,768]{2,1,0:T(8,128)(2,1)} %param.31) | copy-start | bytes 4538884
  1.8 9.9 %collective-permute-start.6 = (bf16[96,768]{1,0:T(8,128)(2,1)S(1)}, bf16[96,768]{1,0:T(8,128)(2,1)}, u32[]{:S(2)}, u32[]{:S(2)}) collective-permute-start(bf16[96,768]{1,0:T(8,128)(2,1)S(1)} %dynamic-slice_bitcast_fusion.14), channel_id=1, source_target_pairs={{0,2},{1,3},{2,0},{3,1},{4,6},{5,7},{6,4},{7,5},{8,10},{9,11},{10,... | collective-permute-start | bytes 442376 | tf_op jit(solution)/shard_map/ppermute | solution.py:18
  5.8 39.3 %collective-permute-start.1 = (bf16[96,2304]{1,0:T(8,128)(2,1)S(1)}, bf16[96,2304]{1,0:T(8,128)(2,1)}, u32[]{:S(2)}, u32[]{:S(2)}) collective-permute-start(bf16[96,2304]{1,0:T(8,128)(2,1)S(1)} %dynamic-slice_bitcast_fusion.9), channel_id=1, source_target_pairs={{0,2},{1,3},{2,0},{3,1},{4,6},{5,7},{6,4},{7,5},{8,10},{9,11},{10,... | collective-permute-start | bytes 1327112 | tf_op jit(solution)/shard_map/ppermute | solution.py:18
  7.8 39.0 %collective-permute-start.11 = (bf16[96,3072]{1,0:T(8,128)(2,1)}, bf16[96,3072]{1,0:T(8,128)(2,1)}, u32[]{:S(2)}, u32[]{:S(2)}) collective-permute-start(bf16[96,3072]{1,0:T(8,128)(2,1)} %dynamic-slice_bitcast_fusion.7), channel_id=1, source_target_pairs={{0,2},{1,3},{2,0},{3,1},{4,6},{5,7},{6,4},{7,5},{8,10},{9,11},{10,... | collective-permute-start | bytes 1769480 | tf_op jit(solution)/shard_map/ppermute | solution.py:18
  10.8 53.0 %copy-start.2 = (bf16[5,197,768]{2,1,0:T(8,128)(2,1)S(1)}, bf16[5,197,768]{2,1,0:T(8,128)(2,1)}, u32[]{:S(2)}) copy-start(bf16[5,197,768]{2,1,0:T(8,128)(2,1)} %param.16) | copy-start | bytes 4538884
  10.8 36.5 %collective-permute-start.16 = (bf16[384,768]{1,0:T(8,128)(2,1)}, bf16[384,768]{1,0:T(8,128)(2,1)}, u32[]{:S(2)}, u32[]{:S(2)}) collective-permute-start(bf16[384,768]{1,0:T(8,128)(2,1)} %dynamic-slice_bitcast_fusion.6), channel_id=1, source_target_pairs={{0,2},{1,3},{2,0},{3,1},{4,6},{5,7},{6,4},{7,5},{8,10},{9,11},{10,... | collective-permute-start | bytes 1769480 | tf_op jit(solution)/shard_map/ppermute | solution.py:18
  11.6 32.9 %collective-permute-start.8 = (bf16[96,768]{1,0:T(8,128)(2,1)}, bf16[96,768]{1,0:T(8,128)(2,1)}, u32[]{:S(2)}, u32[]{:S(2)}) collective-permute-start(bf16[96,768]{1,0:T(8,128)(2,1)} %collective-permute-done.6.refs_8_.refs_19_), channel_id=1, source_target_pairs={{0,1},{1,0},{2,3},{3,2},{4,5},{5,4},{6,7},{7,6},{8,9},{9,8},{10,11... | collective-permute-start | bytes 442376 | tf_op jit(solution)/shard_map/ppermute | solution.py:18
  11.7 33.2 %collective-permute-start.7 = (bf16[96,768]{1,0:T(8,128)(2,1)}, bf16[96,768]{1,0:T(8,128)(2,1)}, u32[]{:S(2)}, u32[]{:S(2)}) collective-permute-start(bf16[96,768]{1,0:T(8,128)(2,1)} %collective-permute-done.6.refs_8_.refs_19_), channel_id=1, source_target_pairs={{0,4},{4,0},{8,12},{12,8},{16,20},{20,16},{24,28},{28,24},{1,5},{5... | collective-permute-start | bytes 442376 | tf_op jit(solution)/shard_map/ppermute | solution.py:18
  44.5 2.7 collective-permute-start.5
  44.9 22.5 %collective-permute-start = (bf16[192,2304]{1,0:T(8,128)(2,1)}, bf16[192,2304]{1,0:T(8,128)(2,1)}, u32[]{:S(2)}, u32[]{:S(2)}) collective-permute-start(bf16[192,2304]{1,0:T(8,128)(2,1)} %refs_5_.5), channel_id=1, source_target_pairs={{0,1},{1,0},{2,3},{3,2},{4,5},{5,4},{6,7},{7,6},{8,9},{9,8},{10,11... | collective-permute-start | bytes 2654216 | tf_op jit(solution)/shard_map/ppermute | solution.py:18
  45.1 13.3 %collective-permute-start.2 = (bf16[96,2304]{1,0:T(8,128)(2,1)}, bf16[96,2304]{1,0:T(8,128)(2,1)}, u32[]{:S(2)}, u32[]{:S(2)}) collective-permute-start(bf16[96,2304]{1,0:T(8,128)(2,1)} %collective-permute-done.1.refs_7_), channel_id=1, source_target_pairs={{0,4},{4,0},{8,12},{12,8},{16,20},{20,16},{24,28},{28,24},{1,5},{5... | collective-permute-start | bytes 1327112 | tf_op jit(solution)/shard_map/ppermute | solution.py:18
  46.9 23.6 %collective-permute-start.12 = (bf16[96,3072]{1,0:T(8,128)(2,1)}, bf16[96,3072]{1,0:T(8,128)(2,1)}, u32[]{:S(2)}, u32[]{:S(2)}) collective-permute-start(bf16[96,3072]{1,0:T(8,128)(2,1)} %collective-permute-done.11.refs_5_.refs_13_), channel_id=1, source_target_pairs={{0,4},{4,0},{8,12},{12,8},{16,20},{20,16},{24,28},{28,24},{1,5},{5... | collective-permute-start | bytes 1769480 | tf_op jit(solution)/shard_map/ppermute | solution.py:18
  47.2 51.7 %collective-permute-start.10 = (bf16[192,3072]{1,0:T(8,128)(2,1)}, bf16[192,3072]{1,0:T(8,128)(2,1)}, u32[]{:S(2)}, u32[]{:S(2)}) collective-permute-start(bf16[192,3072]{1,0:T(8,128)(2,1)} %refs_11_.1), channel_id=1, source_target_pairs={{0,1},{1,0},{2,3},{3,2},{4,5},{5,4},{6,7},{7,6},{8,9},{9,8},{10,11... | collective-permute-start | bytes 3538952 | tf_op jit(solution)/shard_map/ppermute | solution.py:18
  47.3 19.6 %collective-permute-start.3 = (bf16[96,2304]{1,0:T(8,128)(2,1)}, bf16[96,2304]{1,0:T(8,128)(2,1)}, u32[]{:S(2)}, u32[]{:S(2)}) collective-permute-start(bf16[96,2304]{1,0:T(8,128)(2,1)} %collective-permute-done.1.refs_7_), channel_id=1, source_target_pairs={{0,1},{1,0},{2,3},{3,2},{4,5},{5,4},{6,7},{7,6},{8,9},{9,8},{10,11... | collective-permute-start | bytes 1327112 | tf_op jit(solution)/shard_map/ppermute | solution.py:18
  58.4 13.8 %collective-permute-start.4 = (bf16[96,2304]{1,0:T(8,128)(2,1)}, bf16[96,2304]{1,0:T(8,128)(2,1)}, u32[]{:S(2)}, u32[]{:S(2)}) collective-permute-start(bf16[96,2304]{1,0:T(8,128)(2,1)} %collective-permute-done.2.refs_8_), channel_id=1, source_target_pairs={{0,1},{1,0},{2,3},{3,2},{4,5},{5,4},{6,7},{7,6},{8,9},{9,8},{10,11... | collective-permute-start | bytes 1327112 | tf_op jit(solution)/shard_map/ppermute | solution.py:18
  66.9 15.4 %copy-start.5 = (bf16[768,768]{1,0:T(8,128)(2,1)S(1)}, bf16[768,768]{1,0:T(8,128)(2,1)}, u32[]{:S(2)}) copy-start(bf16[768,768]{1,0:T(8,128)(2,1)} %refs_5_.4) | copy-start | bytes 3538948
  66.9 15.4 %collective-permute-start.9 = (bf16[96,768]{1,0:T(8,128)(2,1)}, bf16[96,768]{1,0:T(8,128)(2,1)S(1)}, u32[]{:S(2)}, u32[]{:S(2)}) collective-permute-start(bf16[96,768]{1,0:T(8,128)(2,1)} %collective-permute-done.7.refs_9_.refs_20_), channel_id=1, source_target_pairs={{0,1},{1,0},{2,3},{3,2},{4,5},{5,4},{6,7},{7,6},{8,9},{9,8},{10,11... | collective-permute-start | bytes 442376 | tf_op jit(solution)/shard_map/ppermute | solution.py:18
  67.4 30.9 %collective-permute-start.13 = (bf16[96,3072]{1,0:T(8,128)(2,1)}, bf16[96,3072]{1,0:T(8,128)(2,1)S(1)}, u32[]{:S(2)}, u32[]{:S(2)}) collective-permute-start(bf16[96,3072]{1,0:T(8,128)(2,1)} %collective-permute-done.11.refs_5_.refs_13_), channel_id=1, source_target_pairs={{0,1},{1,0},{2,3},{3,2},{4,5},{5,4},{6,7},{7,6},{8,9},{9,8},{10,11... | collective-permute-start | bytes 1769480 | tf_op jit(solution)/shard_map/ppermute | solution.py:18
  70.4 28.4 %collective-permute-start.17 = (bf16[384,768]{1,0:T(8,128)(2,1)}, bf16[384,768]{1,0:T(8,128)(2,1)S(1)}, u32[]{:S(2)}, u32[]{:S(2)}) collective-permute-start(bf16[384,768]{1,0:T(8,128)(2,1)} %collective-permute-done.16.refs_6_.refs_7_), channel_id=1, source_target_pairs={{0,4},{4,0},{8,12},{12,8},{16,20},{20,16},{24,28},{28,24},{1,5},{5... | collective-permute-start | bytes 1769480 | tf_op jit(solution)/shard_map/ppermute | solution.py:18
  72.1 26.8 %collective-permute-start.14 = (bf16[96,3072]{1,0:T(8,128)(2,1)}, bf16[96,3072]{1,0:T(8,128)(2,1)S(1)}, u32[]{:S(2)}, u32[]{:S(2)}) collective-permute-start(bf16[96,3072]{1,0:T(8,128)(2,1)} %collective-permute-done.12.refs_6_.refs_14_), channel_id=1, source_target_pairs={{0,1},{1,0},{2,3},{3,2},{4,5},{5,4},{6,7},{7,6},{8,9},{9,8},{10,11... | collective-permute-start | bytes 1769480 | tf_op jit(solution)/shard_map/ppermute | solution.py:18
  82.4 45.4 %collective-permute-start.15 = (bf16[768,768]{1,0:T(8,128)(2,1)S(1)}, bf16[768,768]{1,0:T(8,128)(2,1)S(1)}, u32[]{:S(2)}, u32[]{:S(2)}) collective-permute-start(bf16[768,768]{1,0:T(8,128)(2,1)S(1)} %copy-done.5), channel_id=1, source_target_pairs={{0,1},{1,0},{2,3},{3,2},{4,5},{5,4},{6,7},{7,6},{8,9},{9,8},{10,11... | collective-permute-start | bytes 3538952 | tf_op jit(solution)/shard_map/ppermute | solution.py:18
  98.3 29.5 %collective-permute-start.18 = (bf16[384,768]{1,0:T(8,128)(2,1)}, bf16[384,768]{1,0:T(8,128)(2,1)S(1)}, u32[]{:S(2)}, u32[]{:S(2)}) collective-permute-start(bf16[384,768]{1,0:T(8,128)(2,1)} %collective-permute-done.16.refs_6_.refs_7_), channel_id=1, source_target_pairs={{0,1},{1,0},{2,3},{3,2},{4,5},{5,4},{6,7},{7,6},{8,9},{9,8},{10,11... | collective-permute-start | bytes 1769480 | tf_op jit(solution)/shard_map/ppermute | solution.py:18
  98.8 17.9 %copy-start.20 = (bf16[384,768]{1,0:T(8,128)(2,1)}, bf16[384,768]{1,0:T(8,128)(2,1)S(1)}, u32[]{:S(2)}) copy-start(bf16[384,768]{1,0:T(8,128)(2,1)S(1)} %collective-permute-done.17.refs_7_.refs_8_) | copy-start | bytes 1769476
  98.8 28.9 %collective-permute-start.19 = (bf16[384,768]{1,0:T(8,128)(2,1)S(1)}, bf16[384,768]{1,0:T(8,128)(2,1)S(1)}, u32[]{:S(2)}, u32[]{:S(2)}) collective-permute-start(bf16[384,768]{1,0:T(8,128)(2,1)S(1)} %collective-permute-done.17.refs_7_.refs_8_), channel_id=1, source_target_pairs={{0,1},{1,0},{2,3},{3,2},{4,5},{5,4},{6,7},{7,6},{8,9},{9,8},{10,11... | collective-permute-start | bytes 1769480 | tf_op jit(solution)/shard_map/ppermute | solution.py:18
  181.4 14.6 %copy-start.10 = (f32[1,768]{1,0:T(1,128)S(1)}, f32[1,768]{1,0:T(1,128)}, u32[]{:S(2)}) copy-start(f32[1,768]{1,0:T(1,128)} %get-tuple-element.48) | copy-start | bytes 9220
  181.4 14.7 %copy-start.9 = (f32[1,768]{1,0:T(1,128)S(1)}, f32[1,768]{1,0:T(1,128)}, u32[]{:S(2)}) copy-start(f32[1,768]{1,0:T(1,128)} %get-tuple-element.49) | copy-start | bytes 9220
  181.4 14.8 %copy-start.8 = (f32[1,768]{1,0:T(1,128)S(1)}, f32[1,768]{1,0:T(1,128)}, u32[]{:S(2)}) copy-start(f32[1,768]{1,0:T(1,128)} %get-tuple-element.50) | copy-start | bytes 9220
  181.4 14.9 %copy-start.7 = (f32[1,768]{1,0:T(1,128)S(1)}, f32[1,768]{1,0:T(1,128)}, u32[]{:S(2)}) copy-start(f32[1,768]{1,0:T(1,128)} %get-tuple-element.51) | copy-start | bytes 9220
  181.4 15.5 %copy-start.6 = (f32[1,3072]{1,0:T(1,128)S(1)}, f32[1,3072]{1,0:T(1,128)}, u32[]{:S(2)}) copy-start(f32[1,3072]{1,0:T(1,128)} %get-tuple-element.52) | copy-start | bytes 36868
  181.4 16.7 %copy-start.27 = (bf16[5,208,768]{2,1,0:T(8,128)(2,1)S(1)}, bf16[5,208,768]{2,1,0:T(8,128)(2,1)}, u32[]{:S(2)}) copy-start(bf16[5,208,768]{2,1,0:T(8,128)(2,1)} %get-tuple-element.54) | copy-start | bytes 4792324
  181.4 16.7 %copy-start.28 = (bf16[5,208,768]{2,1,0:T(8,128)(2,1)S(1)}, bf16[5,208,768]{2,1,0:T(8,128)(2,1)}, u32[]{:S(2)}) copy-start(bf16[5,208,768]{2,1,0:T(8,128)(2,1)} %get-tuple-element.55) | copy-start | bytes 4792324
  197.7 9.8 %collective-permute-start.20 = (f32[2,1,18,128]{3,2,0,1:T(8,128)S(1)}, f32[2,1,18,128]{3,2,0,1:T(8,128)S(1)}, u32[]{:S(2)}, u32[]{:S(2)}) collective-permute-start(f32[2,1,18,128]{3,2,0,1:T(8,128)S(1)} %dynamic-slice_bitcast_fusion.16), channel_id=1, source_target_pairs={{0,1},{1,0},{2,3},{3,2},{4,5},{5,4},{6,7},{7,6},{8,9},{9,8},{10,11... | collective-permute-start | bytes 55304 | tf_op jit(solution)/shard_map/ppermute | solution.py:18
  200.0 20.5 %collective-permute-start.32 = (bf16[2,192,768]{2,1,0:T(8,128)(2,1)S(1)}, bf16[2,192,768]{2,1,0:T(8,128)(2,1)S(1)}, u32[]{:S(2)}, u32[]{:S(2)}) collective-permute-start(bf16[2,192,768]{2,1,0:T(8,128)(2,1)S(1)} %dynamic-slice_bitcast_fusion.5), channel_id=1, source_target_pairs={{0,1},{1,0},{2,3},{3,2},{4,5},{5,4},{6,7},{7,6},{8,9},{9,8},{10,11... | collective-permute-start | bytes 1769480 | tf_op jit(solution)/shard_map/ppermute | solution.py:18
  207.4 47.9 %collective-permute-start.25 = (bf16[2,192,2304]{2,1,0:T(8,128)(2,1)}, bf16[2,192,2304]{2,1,0:T(8,128)(2,1)}, u32[]{:S(2)}, u32[]{:S(2)}) collective-permute-start(bf16[2,192,2304]{2,1,0:T(8,128)(2,1)} %dynamic-slice_bitcast_fusion.2), channel_id=1, source_target_pairs={{0,1},{1,0},{2,3},{3,2},{4,5},{5,4},{6,7},{7,6},{8,9},{9,8},{10,11... | collective-permute-start | bytes 5308424 | tf_op jit(solution)/shard_map/ppermute | solution.py:18
  207.6 3.8 collective-permute-start.21
  210.7 48.0 %collective-permute-start.46 = (bf16[2,768,768]{2,1,0:T(8,128)(2,1)}, bf16[2,768,768]{2,1,0:T(8,128)(2,1)}, u32[]{:S(2)}, u32[]{:S(2)}) collective-permute-start(bf16[2,768,768]{2,1,0:T(8,128)(2,1)} %dynamic-slice_bitcast_fusion), channel_id=1, source_target_pairs={{0,1},{1,0},{2,3},{3,2},{4,5},{5,4},{6,7},{7,6},{8,9},{9,8},{10,11... | collective-permute-start | bytes 7077896 | tf_op jit(solution)/shard_map/ppermute | solution.py:18
  211.4 7.3 %collective-permute-start.22 = (f32[1,18,128]{2,1,0:T(8,128)S(1)}, f32[1,18,128]{2,1,0:T(8,128)S(1)}, u32[]{:S(2)}, u32[]{:S(2)}) collective-permute-start(f32[1,18,128]{2,1,0:T(8,128)S(1)} %add_bitcast_fusion), channel_id=1, source_target_pairs={{0,4},{4,0},{8,12},{12,8},{16,20},{20,16},{24,28},{28,24},{1,5},{5... | collective-permute-start | bytes 27656 | tf_op jit(solution)/shard_map/ppermute | solution.py:18
  218.6 5.2 %collective-permute-start.23 = (f32[1,18,128]{2,1,0:T(8,128)S(1)}, f32[1,18,128]{2,1,0:T(8,128)S(1)}, u32[]{:S(2)}, u32[]{:S(2)}) collective-permute-start(f32[1,18,128]{2,1,0:T(8,128)S(1)} %add.168), channel_id=1, source_target_pairs={{0,8},{4,12},{8,0},{12,4},{16,24},{20,28},{24,16},{28,20},{1,9},{5... | collective-permute-start | bytes 27656 | tf_op jit(solution)/shard_map/ppermute | solution.py:18
  220.7 8.3 %collective-permute-start.33 = (bf16[1,192,768]{2,1,0:T(8,128)(2,1)S(1)}, bf16[1,192,768]{2,1,0:T(8,128)(2,1)S(1)}, u32[]{:S(2)}, u32[]{:S(2)}) collective-permute-start(bf16[1,192,768]{2,1,0:T(8,128)(2,1)S(1)} %constant_dynamic-slice_fusion.2), channel_id=1, source_target_pairs={{0,2},{1,3},{2,0},{3,1},{4,6},{5,7},{6,4},{7,5},{8,10},{9,11},{10,... | collective-permute-start | bytes 884744 | tf_op jit(solution)/shard_map/ppermute | solution.py:18
  223.9 38.2 %collective-permute-start.39 = (bf16[2,192,3072]{2,1,0:T(8,128)(2,1)}, bf16[2,192,3072]{2,1,0:T(8,128)(2,1)}, u32[]{:S(2)}, u32[]{:S(2)}) collective-permute-start(bf16[2,192,3072]{2,1,0:T(8,128)(2,1)} %dynamic-slice_bitcast_fusion.1), channel_id=1, source_target_pairs={{0,1},{1,0},{2,3},{3,2},{4,5},{5,4},{6,7},{7,6},{8,9},{9,8},{10,11... | collective-permute-start | bytes 7077896 | tf_op jit(solution)/shard_map/ppermute | solution.py:18
  223.9 19.6 %collective-permute-start.24 = (f32[1,18,128]{2,1,0:T(8,128)S(1)}, f32[1,18,128]{2,1,0:T(8,128)S(1)}, u32[]{:S(2)}, u32[]{:S(2)}) collective-permute-start(f32[1,18,128]{2,1,0:T(8,128)S(1)} %add.169), channel_id=1, source_target_pairs={{0,16},{4,20},{8,24},{12,28},{16,0},{20,4},{24,8},{28,12},{1,17},{... | collective-permute-start | bytes 27656 | tf_op jit(solution)/shard_map/ppermute | solution.py:18
  230.5 13.0 %collective-permute-start.34 = (bf16[96,768]{1,0:T(8,128)(2,1)}, bf16[96,768]{1,0:T(8,128)(2,1)}, u32[]{:S(2)}, u32[]{:S(2)}) collective-permute-start(bf16[96,768]{1,0:T(8,128)(2,1)} %dynamic-slice_bitcast_fusion.13), channel_id=1, source_target_pairs={{0,4},{4,0},{8,12},{12,8},{16,20},{20,16},{24,28},{28,24},{1,5},{5... | collective-permute-start | bytes 442376 | tf_op jit(solution)/shard_map/ppermute | solution.py:18
  244.6 4.4 %collective-permute-start.35 = (bf16[48,768]{1,0:T(8,128)(2,1)S(1)}, bf16[48,768]{1,0:T(8,128)(2,1)S(1)}, u32[]{:S(2)}, u32[]{:S(2)}) collective-permute-start(bf16[48,768]{1,0:T(8,128)(2,1)S(1)} %dynamic-slice_bitcast_fusion.15), channel_id=1, source_target_pairs={{0,8},{4,12},{8,0},{12,4},{16,24},{20,28},{24,16},{28,20},{1,9},{5... | collective-permute-start | bytes 221192 | tf_op jit(solution)/shard_map/ppermute | solution.py:18
  249.0 6.1 %collective-permute-start.36 = (bf16[48,768]{1,0:T(8,128)(2,1)S(1)}, bf16[48,768]{1,0:T(8,128)(2,1)S(1)}, u32[]{:S(2)}, u32[]{:S(2)}) collective-permute-start(bf16[48,768]{1,0:T(8,128)(2,1)S(1)} %fusion.15), channel_id=1, source_target_pairs={{0,16},{4,20},{8,24},{12,28},{16,0},{20,4},{24,8},{28,12},{1,17},{... | collective-permute-start | bytes 221192 | tf_op jit(solution)/shard_map/ppermute | solution.py:18
  255.2 27.2 %collective-permute-start.37 = (bf16[48,768]{1,0:T(8,128)(2,1)S(1)}, bf16[48,768]{1,0:T(8,128)(2,1)S(1)}, u32[]{:S(2)}, u32[]{:S(2)}) collective-permute-start(bf16[48,768]{1,0:T(8,128)(2,1)S(1)} %add_convert_fusion.7), channel_id=1, source_target_pairs={{0,8},{4,12},{8,0},{12,4},{16,24},{20,28},{24,16},{28,20},{1,9},{5... | collective-permute-start | bytes 221192 | tf_op jit(solution)/shard_map/ppermute | solution.py:18
  257.2 22.6 %collective-permute-start.26 = (bf16[1,192,2304]{2,1,0:T(8,128)(2,1)S(1)}, bf16[1,192,2304]{2,1,0:T(8,128)(2,1)S(1)}, u32[]{:S(2)}, u32[]{:S(2)}) collective-permute-start(bf16[1,192,2304]{2,1,0:T(8,128)(2,1)S(1)} %constant_dynamic-slice_fusion.3), channel_id=1, source_target_pairs={{0,2},{1,3},{2,0},{3,1},{4,6},{5,7},{6,4},{7,5},{8,10},{9,11},{10,... | collective-permute-start | bytes 2654216 | tf_op jit(solution)/shard_map/ppermute | solution.py:18
  261.0 44.1 %collective-permute-start.47 = (bf16[1,768,768]{2,1,0:T(8,128)(2,1)S(1)}, bf16[1,768,768]{2,1,0:T(8,128)(2,1)S(1)}, u32[]{:S(2)}, u32[]{:S(2)}) collective-permute-start(bf16[1,768,768]{2,1,0:T(8,128)(2,1)S(1)} %constant_dynamic-slice_fusion), channel_id=1, source_target_pairs={{0,2},{1,3},{2,0},{3,1},{4,6},{5,7},{6,4},{7,5},{8,10},{9,11},{10,... | collective-permute-start | bytes 3538952 | tf_op jit(solution)/shard_map/ppermute | solution.py:18
  280.1 8.4 %collective-permute-start.27 = (bf16[96,2304]{1,0:T(8,128)(2,1)S(1)}, bf16[96,2304]{1,0:T(8,128)(2,1)S(1)}, u32[]{:S(2)}, u32[]{:S(2)}) collective-permute-start(bf16[96,2304]{1,0:T(8,128)(2,1)S(1)} %dynamic-slice_bitcast_fusion.8), channel_id=1, source_target_pairs={{0,4},{4,0},{8,12},{12,8},{16,20},{20,16},{24,28},{28,24},{1,5},{5... | collective-permute-start | bytes 1327112 | tf_op jit(solution)/shard_map/ppermute | solution.py:18
  280.8 44.3 %collective-permute-start.40 = (bf16[1,192,3072]{2,1,0:T(8,128)(2,1)S(1)}, bf16[1,192,3072]{2,1,0:T(8,128)(2,1)S(1)}, u32[]{:S(2)}, u32[]{:S(2)}) collective-permute-start(bf16[1,192,3072]{2,1,0:T(8,128)(2,1)S(1)} %constant_dynamic-slice_fusion.1), channel_id=1, source_target_pairs={{0,2},{1,3},{2,0},{3,1},{4,6},{5,7},{6,4},{7,5},{8,10},{9,11},{10,... | collective-permute-start | bytes 3538952 | tf_op jit(solution)/shard_map/ppermute | solution.py:18
  282.4 99.1 %collective-permute-start.38 = (bf16[96,768]{1,0:T(8,128)(2,1)S(1)}, bf16[96,768]{1,0:T(8,128)(2,1)S(1)}, u32[]{:S(2)}, u32[]{:S(2)}) collective-permute-start(bf16[96,768]{1,0:T(8,128)(2,1)S(1)} %maximum_select_fusion.7), channel_id=1, source_target_pairs={{0,4},{4,0},{8,12},{12,8},{16,20},{20,16},{24,28},{28,24},{1,5},{5... | collective-permute-start | bytes 442376 | tf_op jit(solution)/shard_map/ppermute | solution.py:18
  305.5 22.6 %collective-permute-start.48 = (bf16[384,768]{1,0:T(8,128)(2,1)S(1)}, bf16[384,768]{1,0:T(8,128)(2,1)S(1)}, u32[]{:S(2)}, u32[]{:S(2)}) collective-permute-start(bf16[384,768]{1,0:T(8,128)(2,1)S(1)} %dynamic-slice_bitcast_fusion.3), channel_id=1, source_target_pairs={{0,4},{4,0},{8,12},{12,8},{16,20},{20,16},{24,28},{28,24},{1,5},{5... | collective-permute-start | bytes 1769480 | tf_op jit(solution)/shard_map/ppermute | solution.py:18
  325.6 10.1 %collective-permute-start.41 = (bf16[96,3072]{1,0:T(8,128)(2,1)S(1)}, bf16[96,3072]{1,0:T(8,128)(2,1)S(1)}, u32[]{:S(2)}, u32[]{:S(2)}) collective-permute-start(bf16[96,3072]{1,0:T(8,128)(2,1)S(1)} %dynamic-slice_bitcast_fusion.4), channel_id=1, source_target_pairs={{0,4},{4,0},{8,12},{12,8},{16,20},{20,16},{24,28},{28,24},{1,5},{5... | collective-permute-start | bytes 1769480 | tf_op jit(solution)/shard_map/ppermute | solution.py:18
  326.4 11.2 %collective-permute-start.28 = (bf16[48,2304]{1,0:T(8,128)(2,1)S(1)}, bf16[48,2304]{1,0:T(8,128)(2,1)S(1)}, u32[]{:S(2)}, u32[]{:S(2)}) collective-permute-start(bf16[48,2304]{1,0:T(8,128)(2,1)S(1)} %dynamic-slice_bitcast_fusion.12), channel_id=1, source_target_pairs={{0,8},{4,12},{8,0},{12,4},{16,24},{20,28},{24,16},{28,20},{1,9},{5... | collective-permute-start | bytes 663560 | tf_op jit(solution)/shard_map/ppermute | solution.py:18
  328.4 17.6 %collective-permute-start.49 = (bf16[192,768]{1,0:T(8,128)(2,1)S(1)}, bf16[192,768]{1,0:T(8,128)(2,1)S(1)}, u32[]{:S(2)}, u32[]{:S(2)}) collective-permute-start(bf16[192,768]{1,0:T(8,128)(2,1)S(1)} %dynamic-slice_bitcast_fusion.10), channel_id=1, source_target_pairs={{0,8},{4,12},{8,0},{12,4},{16,24},{20,28},{24,16},{28,20},{1,9},{5... | collective-permute-start | bytes 884744 | tf_op jit(solution)/shard_map/ppermute | solution.py:18
  335.9 13.8 %collective-permute-start.42 = (bf16[48,3072]{1,0:T(8,128)(2,1)S(1)}, bf16[48,3072]{1,0:T(8,128)(2,1)S(1)}, u32[]{:S(2)}, u32[]{:S(2)}) collective-permute-start(bf16[48,3072]{1,0:T(8,128)(2,1)S(1)} %dynamic-slice_bitcast_fusion.11), channel_id=1, source_target_pairs={{0,8},{4,12},{8,0},{12,4},{16,24},{20,28},{24,16},{28,20},{1,9},{5... | collective-permute-start | bytes 884744 | tf_op jit(solution)/shard_map/ppermute | solution.py:18
  337.6 13.6 %collective-permute-start.29 = (bf16[48,2304]{1,0:T(8,128)(2,1)S(1)}, bf16[48,2304]{1,0:T(8,128)(2,1)S(1)}, u32[]{:S(2)}, u32[]{:S(2)}) collective-permute-start(bf16[48,2304]{1,0:T(8,128)(2,1)S(1)} %fusion.12), channel_id=1, source_target_pairs={{0,16},{4,20},{8,24},{12,28},{16,0},{20,4},{24,8},{28,12},{1,17},{... | collective-permute-start | bytes 663560 | tf_op jit(solution)/shard_map/ppermute | solution.py:18
  346.0 20.9 %collective-permute-start.50 = (bf16[192,768]{1,0:T(8,128)(2,1)S(1)}, bf16[192,768]{1,0:T(8,128)(2,1)S(1)}, u32[]{:S(2)}, u32[]{:S(2)}) collective-permute-start(bf16[192,768]{1,0:T(8,128)(2,1)S(1)} %fusion.10), channel_id=1, source_target_pairs={{0,16},{4,20},{8,24},{12,28},{16,0},{20,4},{24,8},{28,12},{1,17},{... | collective-permute-start | bytes 884744 | tf_op jit(solution)/shard_map/ppermute | solution.py:18
  349.8 20.3 %collective-permute-start.43 = (bf16[48,3072]{1,0:T(8,128)(2,1)S(1)}, bf16[48,3072]{1,0:T(8,128)(2,1)S(1)}, u32[]{:S(2)}, u32[]{:S(2)}) collective-permute-start(bf16[48,3072]{1,0:T(8,128)(2,1)S(1)} %fusion.11), channel_id=1, source_target_pairs={{0,16},{4,20},{8,24},{12,28},{16,0},{20,4},{24,8},{28,12},{1,17},{... | collective-permute-start | bytes 884744 | tf_op jit(solution)/shard_map/ppermute | solution.py:18
  351.3 19.0 %collective-permute-start.30 = (bf16[48,2304]{1,0:T(8,128)(2,1)S(1)}, bf16[48,2304]{1,0:T(8,128)(2,1)S(1)}, u32[]{:S(2)}, u32[]{:S(2)}) collective-permute-start(bf16[48,2304]{1,0:T(8,128)(2,1)S(1)} %add_convert_fusion.6), channel_id=1, source_target_pairs={{0,8},{4,12},{8,0},{12,4},{16,24},{20,28},{24,16},{28,20},{1,9},{5... | collective-permute-start | bytes 663560 | tf_op jit(solution)/shard_map/ppermute | solution.py:18
  367.0 9.4 %collective-permute-start.51 = (bf16[192,768]{1,0:T(8,128)(2,1)S(1)}, bf16[192,768]{1,0:T(8,128)(2,1)S(1)}, u32[]{:S(2)}, u32[]{:S(2)}) collective-permute-start(bf16[192,768]{1,0:T(8,128)(2,1)S(1)} %add_convert_fusion.3), channel_id=1, source_target_pairs={{0,8},{4,12},{8,0},{12,4},{16,24},{20,28},{24,16},{28,20},{1,9},{5... | collective-permute-start | bytes 884744 | tf_op jit(solution)/shard_map/ppermute | solution.py:18
  370.2 9.4 %collective-permute-start.44 = (bf16[48,3072]{1,0:T(8,128)(2,1)S(1)}, bf16[48,3072]{1,0:T(8,128)(2,1)S(1)}, u32[]{:S(2)}, u32[]{:S(2)}) collective-permute-start(bf16[48,3072]{1,0:T(8,128)(2,1)S(1)} %add_convert_fusion.4), channel_id=1, source_target_pairs={{0,8},{4,12},{8,0},{12,4},{16,24},{20,28},{24,16},{28,20},{1,9},{5... | collective-permute-start | bytes 884744 | tf_op jit(solution)/shard_map/ppermute | solution.py:18
  370.4 13.2 %collective-permute-start.31 = (bf16[96,2304]{1,0:T(8,128)(2,1)S(1)}, bf16[96,2304]{1,0:T(8,128)(2,1)S(1)}, u32[]{:S(2)}, u32[]{:S(2)}) collective-permute-start(bf16[96,2304]{1,0:T(8,128)(2,1)S(1)} %maximum_select_fusion.5), channel_id=1, source_target_pairs={{0,4},{4,0},{8,12},{12,8},{16,20},{20,16},{24,28},{28,24},{1,5},{5... | collective-permute-start | bytes 1327112 | tf_op jit(solution)/shard_map/ppermute | solution.py:18
  376.6 19.6 %collective-permute-start.52 = (bf16[384,768]{1,0:T(8,128)(2,1)S(1)}, bf16[384,768]{1,0:T(8,128)(2,1)S(1)}, u32[]{:S(2)}, u32[]{:S(2)}) collective-permute-start(bf16[384,768]{1,0:T(8,128)(2,1)S(1)} %maximum_select_fusion.4), channel_id=1, source_target_pairs={{0,4},{4,0},{8,12},{12,8},{16,20},{20,16},{24,28},{28,24},{1,5},{5... | collective-permute-start | bytes 1769480 | tf_op jit(solution)/shard_map/ppermute | solution.py:18
  379.7 25.0 %collective-permute-start.45 = (bf16[96,3072]{1,0:T(8,128)(2,1)S(1)}, bf16[96,3072]{1,0:T(8,128)(2,1)S(1)}, u32[]{:S(2)}, u32[]{:S(2)}) collective-permute-start(bf16[96,3072]{1,0:T(8,128)(2,1)S(1)} %maximum_select_fusion.3), channel_id=1, source_target_pairs={{0,4},{4,0},{8,12},{12,8},{16,20},{20,16},{24,28},{28,24},{1,5},{5... | collective-permute-start | bytes 1769480 | tf_op jit(solution)/shard_map/ppermute | solution.py:18
  (26 other events, 105.3 us)
